TPU v7x, 32 devices: a whole 2x2x4 slice. The times are simulated.
32 devices in a mesh: space: 16 (over z, x, core), shot: 2 (over y).
Axes of the slice: x: 2, y: 2, z: 4, core: 2. Of those that a mesh axis runs over, the one named last changes fastest.
Arguments:
- courant: float32 [256, 64, 128], P('space'), may hold values from 0.15 to 0.42
- p_current: float32 [2, 256, 64, 128], P('shot', 'space'), may hold values from -6 to 6
- p_later: float32 [2, 256, 64, 128], P('shot', 'space'), may hold values from -6 to 6
- q_current: float32 [2, 256, 64, 128], P('shot', 'space'), may hold values from -6 to 6
- q_later: float32 [2, 256, 64, 128], P('shot', 'space'), may hold values from -6 to 6
- wavelet: float32 [2, 6], P('shot'), may hold values from -24 to 24
- source_cell: int32 [2], P('shot'), may hold values from 0 to 2097151
- receiver_cells: int32 [2, 256], P('shot'), may hold values from 0 to 2097151
- residual_data: float32 [2, 6, 256], P('shot'), may hold values from -6 to 6
Outputs:
- gradient: float32 [256, 64, 128], P('space', 'shot')
- q_final: float32 [2, 256, 64, 128], P('shot', 'space')
Inputs may be any that keep to these rules, and one draw needn't show every extreme that they name: `source_cell`: a flat cell index of the whole grid. `receiver_cells`: flat cell indices of the whole grid; cells may repeat.
All inputs are finite; a program needn't handle non-finite values.
Results may differ from a plain program's by a relative error of at most 0.0003.
Values sent between devices are 32-bit elements; how exact they have to be, the bound alone decides.
A program may use at most 64 MiB of HBM per device.

v0:
```python
import jax
import jax.numpy as jnp
from jax import lax
from jax.sharding import PartitionSpec as P

STEPS = 6


coefs = (-205.0 / 72.0, 8.0 / 5.0, -1.0 / 5.0, 8.0 / 315.0, -1.0 / 560.0)


def extended(value, sides, width):
    for axis, dim in sides:
        count, length = (lax.axis_size(axis), value.shape[dim])
        up = [(i, (i + 1) % count) for i in range(count - 1)]
        down = [(j, i) for i, j in up]
        last = lax.slice_in_dim(value, length - width, length, axis=dim)
        leading = lax.slice_in_dim(value, 0, width, axis=dim)
        before = lax.ppermute(last, axis, up)
        after = lax.ppermute(leading, axis, down)
        value = jnp.concatenate([before, value, after], axis=dim)
    return value


def laplace_rows(field):
    extent = field.shape[0]
    core = field[4 : extent - 4]
    total = 3.0 * coefs[0] * core
    for j in range(1, 5):
        total = total + coefs[j] * (field[4 + j : extent - 4 + j] + field[4 - j : extent - 4 - j])
    width_y = core.shape[1]
    padded_y = jnp.pad(core, ((0, 0), (4, 4), (0, 0)))
    for j in range(1, 5):
        total = total + coefs[j] * (
            padded_y[:, 4 + j : 4 + j + width_y] + padded_y[:, 4 - j : 4 - j + width_y]
        )
    width_z = core.shape[2]
    padded_z = jnp.pad(core, ((0, 0), (0, 0), (4, 4)))
    for j in range(1, 5):
        total = total + coefs[j] * (
            padded_z[:, :, 4 + j : 4 + j + width_z] + padded_z[:, :, 4 - j : 4 - j + width_z]
        )
    return total


def inject_local(field, first_row, cells, values):
    flat = field.reshape(-1)
    plane = field.shape[1] * field.shape[2]
    local = cells - first_row * plane
    inside = (local >= 0) & (local < flat.shape[0])
    flat = flat.at[jnp.where(inside, local, 0)].add(jnp.where(inside, values, 0.0))
    return flat.reshape(field.shape)


def body(
    courant,
    p_current,
    p_later,
    q_current,
    q_later,
    wavelet,
    source_cell,
    receiver_cells,
    residual_data,
):
    rows = courant.shape[0]
    first = lax.axis_index("space") * rows
    speed2 = courant * courant
    pc, pn, qc, qn = (p_current[0], p_later[0], q_current[0], q_later[0])
    wave = wavelet[0]
    receivers = receiver_cells[0]
    residual = residual_data[0]
    grad = jnp.zeros(pc.shape, jnp.float32)
    for k in range(STEPS):
        both = extended(jnp.stack((pc, qc)), (("space", 1),), 4)
        p_wide, q_wide = (both[0], both[1])
        lp = laplace_rows(p_wide)
        lq = laplace_rows(q_wide)
        grad = grad + qc * lp
        p_new = inject_local(2.0 * pc - pn + speed2 * lp, first, source_cell, wave[k][None])
        q_new = inject_local(2.0 * qc - qn + speed2 * lq, first, receivers, residual[k])
        pn, pc = (pc, p_new)
        qn, qc = (qc, q_new)
    summed = lax.psum_scatter(grad, "shot", scatter_dimension=1, tiled=True)
    gradient = summed * (1.0 / (STEPS * lax.axis_size("shot")))
    return (gradient, qc[None])


def solution(mesh):
    in_specs = (
        P("space", None, None),
        P("shot", "space", None, None),
        P("shot", "space", None, None),
        P("shot", "space", None, None),
        P("shot", "space", None, None),
        P("shot", None),
        P("shot"),
        P("shot", None),
        P("shot", None, None),
    )
    out_specs = (P("space", "shot", None), P("shot", "space", None, None))
    return jax.shard_map(body, mesh=mesh, in_specs=in_specs, out_specs=out_specs, check_vma=False)
```

profile of v0, /device:TPU:10, one launch (start us, length us, event | category | flops | bytes accessed | tf_op | source)
XLA Modules:
  0.0 144.7 jit_solution(11969124850747653930)
XLA Ops:
  8.5 2.1 %collective-permute-start = (f32[2,4,64,128]{3,2,1,0:T(8,128)S(1)}, f32[2,4,64,128]{3,2,1,0:T(8,128)S(1)}, u32[]{:S(2)}, u32[]{:S(2)}) collective-permute-start(f32[2,4,64,128]{3,2,1,0:T(8,128)S(1)} %get-tuple-element.92), channel_id=1, source_target_pairs={{2,0},{4,2},{6,4},{8,6},{10,8},{12,10},{14,12},{16,14},{18,16},{20... | collective-permute-start | bytes 786440 | tf_op jit(solution)/shard_map/ppermute | solution.py:20
  10.6 2.4 %collective-permute-start.1 = (f32[2,4,64,128]{3,2,1,0:T(8,128)S(1)}, f32[2,4,64,128]{3,2,1,0:T(8,128)S(1)}, u32[]{:S(2)}, u32[]{:S(2)}) collective-permute-start(f32[2,4,64,128]{3,2,1,0:T(8,128)S(1)} %get-tuple-element.93), channel_id=1, source_target_pairs={{0,2},{2,4},{4,6},{6,8},{8,10},{10,12},{12,14},{14,16},{16,18},{18... | collective-permute-start | bytes 786440 | tf_op jit(solution)/shard_map/ppermute | solution.py:19
  15.0 5.1 %collective-permute-done.1 = f32[2,4,64,128]{3,2,1,0:T(8,128)S(1)} collective-permute-done((f32[2,4,64,128]{3,2,1,0:T(8,128)S(1)}, f32[2,4,64,128]{3,2,1,0:T(8,128)S(1)}, u32[]{:S(2)}, u32[]{:S(2)}) %collective-permute-start.1) | collective-permute-done | bytes 262176 | tf_op jit(solution)/shard_map/ppermute | solution.py:19
  20.1 3.7 %fusion.468 = (f32[16,64,128]{2,1,0:T(8,128)S(1)}, f32[16,64,128]{2,1,0:T(8,128)}) fusion(f32[1,16,64,128]{3,2,1,0:T(8,128)} %param.21, f32[16,64,128]{2,1,0:T(8,128)S(1)} %copy-done, f32[1,16,64,128]{3,2,1,0:T(8,128)S(1)} %copy-done.9, f32[16,64,128]{2,1,0:T(8,128)S(1)} %bitcast.437, f32[2,16,64,128]{3,2,1,0:T(8,128)S(1)} %constant_dynamic-update-slice_fusion, ...), kind=kLoop, calls=%fused_computation.747 | loop fusion | flops 6553600 | bytes 4718592 | tf_op jit(solution)/shard_map/add | solution.py:80
  25.4 2.4 %fusion.27 = f32[16,64,128]{2,1,0:T(8,128)S(1)} fusion(f32[16,64,128]{2,1,0:T(8,128)S(1)} %bitcast.438, f32[2,16,64,128]{3,2,1,0:T(8,128)S(1)} %constant_dynamic-update-slice_fusion, f32[2,4,64,128]{3,2,1,0:T(8,128)} %copy-done.20, f32[2,4,64,128]{3,2,1,0:T(8,128)S(1)} %collective-permute-done, f32[1,16,64,128]{3,2,1,0:T(8,128)S(1)} %copy-done.21, ...), kind=kLoop, calls=%fused_computation.263 | loop fusion | flops 6553600 | bytes 3670016 | tf_op jit(solution)/shard_map/add | solution.py:81
  27.7 2.5 %scatter_fusion = f32[131072]{0:T(1024)S(1)} fusion(f32[131072]{0:T(1024)S(1)} %bitcast.403, s32[256]{0:T(256)S(1)} %bitcast.441, f32[256]{0:T(256)S(1)} %get-tuple-element.105), kind=kCustom, calls=%fused_computation | custom fusion | flops 256 | bytes 4096 | tf_op jit(solution)/shard_map/scatter-add | solution.py:51
  30.2 1.9 %collective-permute-start.2 = (f32[2,4,64,128]{3,2,1,0:T(8,128)S(1)}, f32[2,4,64,128]{3,2,1,0:T(8,128)S(1)}, u32[]{:S(2)}, u32[]{:S(2)}) collective-permute-start(f32[2,4,64,128]{3,2,1,0:T(8,128)S(1)} %get-tuple-element.90), channel_id=1, source_target_pairs={{2,0},{4,2},{6,4},{8,6},{10,8},{12,10},{14,12},{16,14},{18,16},{20... | collective-permute-start | bytes 786440 | tf_op jit(solution)/shard_map/ppermute | solution.py:20
  32.2 2.5 %collective-permute-start.3 = (f32[2,4,64,128]{3,2,1,0:T(8,128)S(1)}, f32[2,4,64,128]{3,2,1,0:T(8,128)S(1)}, u32[]{:S(2)}, u32[]{:S(2)}) collective-permute-start(f32[2,4,64,128]{3,2,1,0:T(8,128)S(1)} %get-tuple-element.91), channel_id=1, source_target_pairs={{0,2},{2,4},{4,6},{6,8},{8,10},{10,12},{12,14},{14,16},{16,18},{18... | collective-permute-start | bytes 786440 | tf_op jit(solution)/shard_map/ppermute | solution.py:19
  36.0 4.7 %collective-permute-done.3 = f32[2,4,64,128]{3,2,1,0:T(8,128)S(1)} collective-permute-done((f32[2,4,64,128]{3,2,1,0:T(8,128)S(1)}, f32[2,4,64,128]{3,2,1,0:T(8,128)S(1)}, u32[]{:S(2)}, u32[]{:S(2)}) %collective-permute-start.3) | collective-permute-done | bytes 262176 | tf_op jit(solution)/shard_map/ppermute | solution.py:19
  42.2 1.9 %multiply_add_fusion.3 = (f32[16,64,128]{2,1,0:T(8,128)S(1)}, f32[16,64,128]{2,1,0:T(8,128)}) fusion(f32[16,64,128]{2,1,0:T(8,128)S(1)} %bitcast.417, f32[16,64,128]{2,1,0:T(8,128)S(1)} %copy-done, f32[1,16,64,128]{3,2,1,0:T(8,128)S(1)} %copy-done.9, f32[2,20,64,128]{3,2,1,0:T(8,128)S(1)} %get-tuple-element.89, f32[2,20,64,128]{3,2,1,0:T(8,128)S(1)} %get-tuple-element.88), kind=kLoop, calls=%fused_computation.752 | loop fusion | flops 5505024 | bytes 6815744 | tf_op jit(solution)/shard_map/add | solution.py:80
  45.6 2.5 %scatter_fusion.1 = f32[131072]{0:T(1024)S(1)} fusion(f32[131072]{0:T(1024)S(1)} %bitcast.397, s32[256]{0:T(256)S(1)} %bitcast.442, f32[256]{0:T(256)S(1)} %get-tuple-element.104), kind=kCustom, calls=%fused_computation.1 | custom fusion | flops 256 | bytes 4096 | tf_op jit(solution)/shard_map/scatter-add | solution.py:51
  48.2 1.9 %collective-permute-start.4 = (f32[2,4,64,128]{3,2,1,0:T(8,128)S(1)}, f32[2,4,64,128]{3,2,1,0:T(8,128)S(1)}, u32[]{:S(2)}, u32[]{:S(2)}) collective-permute-start(f32[2,4,64,128]{3,2,1,0:T(8,128)S(1)} %get-tuple-element.86), channel_id=1, source_target_pairs={{2,0},{4,2},{6,4},{8,6},{10,8},{12,10},{14,12},{16,14},{18,16},{20... | collective-permute-start | bytes 786440 | tf_op jit(solution)/shard_map/ppermute | solution.py:20
  50.1 2.4 %collective-permute-start.5 = (f32[2,4,64,128]{3,2,1,0:T(8,128)S(1)}, f32[2,4,64,128]{3,2,1,0:T(8,128)S(1)}, u32[]{:S(2)}, u32[]{:S(2)}) collective-permute-start(f32[2,4,64,128]{3,2,1,0:T(8,128)S(1)} %get-tuple-element.87), channel_id=1, source_target_pairs={{0,2},{2,4},{4,6},{6,8},{8,10},{10,12},{12,14},{14,16},{16,18},{18... | collective-permute-start | bytes 786440 | tf_op jit(solution)/shard_map/ppermute | solution.py:19
  54.0 4.8 %collective-permute-done.5 = f32[2,4,64,128]{3,2,1,0:T(8,128)S(1)} collective-permute-done((f32[2,4,64,128]{3,2,1,0:T(8,128)S(1)}, f32[2,4,64,128]{3,2,1,0:T(8,128)S(1)}, u32[]{:S(2)}, u32[]{:S(2)}) %collective-permute-start.5) | collective-permute-done | bytes 262176 | tf_op jit(solution)/shard_map/ppermute | solution.py:19
  60.3 1.9 %multiply_add_fusion.2 = (f32[16,64,128]{2,1,0:T(8,128)S(1)}, f32[16,64,128]{2,1,0:T(8,128)}) fusion(f32[16,64,128]{2,1,0:T(8,128)S(1)} %bitcast.418, f32[16,64,128]{2,1,0:T(8,128)S(1)} %bitcast.427, f32[16,64,128]{2,1,0:T(8,128)S(1)} %copy-done, f32[2,20,64,128]{3,2,1,0:T(8,128)S(1)} %get-tuple-element.85, f32[2,20,64,128]{3,2,1,0:T(8,128)S(1)} %get-tuple-element.84), kind=kLoop, calls=%fused_computation.751 | loop fusion | flops 5505024 | bytes 6815744 | tf_op jit(solution)/shard_map/add | solution.py:80
  63.8 2.7 %scatter_fusion.2 = f32[131072]{0:T(1024)S(1)} fusion(f32[131072]{0:T(1024)S(1)} %bitcast.385, s32[256]{0:T(256)S(1)} %bitcast.443, f32[256]{0:T(256)S(1)} %get-tuple-element.103), kind=kCustom, calls=%fused_computation.2 | custom fusion | flops 256 | bytes 4096 | tf_op jit(solution)/shard_map/scatter-add | solution.py:51
  66.5 1.9 %collective-permute-start.6 = (f32[2,4,64,128]{3,2,1,0:T(8,128)S(1)}, f32[2,4,64,128]{3,2,1,0:T(8,128)S(1)}, u32[]{:S(2)}, u32[]{:S(2)}) collective-permute-start(f32[2,4,64,128]{3,2,1,0:T(8,128)S(1)} %get-tuple-element.82), channel_id=1, source_target_pairs={{2,0},{4,2},{6,4},{8,6},{10,8},{12,10},{14,12},{16,14},{18,16},{20... | collective-permute-start | bytes 786440 | tf_op jit(solution)/shard_map/ppermute | solution.py:20
  68.4 2.4 %collective-permute-start.7 = (f32[2,4,64,128]{3,2,1,0:T(8,128)S(1)}, f32[2,4,64,128]{3,2,1,0:T(8,128)S(1)}, u32[]{:S(2)}, u32[]{:S(2)}) collective-permute-start(f32[2,4,64,128]{3,2,1,0:T(8,128)S(1)} %get-tuple-element.83), channel_id=1, source_target_pairs={{0,2},{2,4},{4,6},{6,8},{8,10},{10,12},{12,14},{14,16},{16,18},{18... | collective-permute-start | bytes 786440 | tf_op jit(solution)/shard_map/ppermute | solution.py:19
  72.3 4.7 %collective-permute-done.7 = f32[2,4,64,128]{3,2,1,0:T(8,128)S(1)} collective-permute-done((f32[2,4,64,128]{3,2,1,0:T(8,128)S(1)}, f32[2,4,64,128]{3,2,1,0:T(8,128)S(1)}, u32[]{:S(2)}, u32[]{:S(2)}) %collective-permute-start.7) | collective-permute-done | bytes 262176 | tf_op jit(solution)/shard_map/ppermute | solution.py:19
  78.5 2.0 %multiply_add_fusion.1 = (f32[16,64,128]{2,1,0:T(8,128)S(1)}, f32[16,64,128]{2,1,0:T(8,128)}) fusion(f32[16,64,128]{2,1,0:T(8,128)S(1)} %bitcast.428, f32[16,64,128]{2,1,0:T(8,128)S(1)} %bitcast.422, f32[16,64,128]{2,1,0:T(8,128)S(1)} %copy-done, f32[2,20,64,128]{3,2,1,0:T(8,128)S(1)} %get-tuple-element.81, f32[2,20,64,128]{3,2,1,0:T(8,128)S(1)} %get-tuple-element.80), kind=kLoop, calls=%fused_computation.750 | loop fusion | flops 5505024 | bytes 6815744 | tf_op jit(solution)/shard_map/add | solution.py:80
  82.7 2.5 %scatter_fusion.3 = f32[131072]{0:T(1024)S(1)} fusion(f32[131072]{0:T(1024)S(1)} %bitcast.391, s32[256]{0:T(256)S(1)} %bitcast.444, f32[256]{0:T(256)S(1)} %get-tuple-element.102), kind=kCustom, calls=%fused_computation.3 | custom fusion | flops 256 | bytes 4096 | tf_op jit(solution)/shard_map/scatter-add | solution.py:51
  88.2 2.4 %collective-permute-start.9 = (f32[2,4,64,128]{3,2,1,0:T(8,128)S(1)}, f32[2,4,64,128]{3,2,1,0:T(8,128)S(1)}, u32[]{:S(2)}, u32[]{:S(2)}) collective-permute-start(f32[2,4,64,128]{3,2,1,0:T(8,128)S(1)} %get-tuple-element.79), channel_id=1, source_target_pairs={{0,2},{2,4},{4,6},{6,8},{8,10},{10,12},{12,14},{14,16},{16,18},{18... | collective-permute-start | bytes 786440 | tf_op jit(solution)/shard_map/ppermute | solution.py:19
  92.1 4.8 %collective-permute-done.9 = f32[2,4,64,128]{3,2,1,0:T(8,128)S(1)} collective-permute-done((f32[2,4,64,128]{3,2,1,0:T(8,128)S(1)}, f32[2,4,64,128]{3,2,1,0:T(8,128)S(1)}, u32[]{:S(2)}, u32[]{:S(2)}) %collective-permute-start.9) | collective-permute-done | bytes 262176 | tf_op jit(solution)/shard_map/ppermute | solution.py:19
  97.2 2.1 %multiply_add_fusion = (f32[16,64,128]{2,1,0:T(8,128)}, f32[16,64,128]{2,1,0:T(8,128)}) fusion(f32[16,64,128]{2,1,0:T(8,128)S(1)} %bitcast.423, f32[16,64,128]{2,1,0:T(8,128)S(1)} %bitcast.432, f32[16,64,128]{2,1,0:T(8,128)S(1)} %copy-done, f32[2,20,64,128]{3,2,1,0:T(8,128)S(1)} %get-tuple-element.77, f32[2,20,64,128]{3,2,1,0:T(8,128)S(1)} %get-tuple-element.76), kind=kLoop, calls=%fused_computation.749 | loop fusion | flops 5505024 | bytes 6815744 | tf_op jit(solution)/shard_map/add | solution.py:80
  100.5 2.5 %scatter_fusion.4 = f32[131072]{0:T(1024)S(1)} fusion(f32[131072]{0:T(1024)S(1)} %bitcast.409, s32[256]{0:T(256)S(1)} %bitcast.445, f32[256]{0:T(256)S(1)} %get-tuple-element.101), kind=kCustom, calls=%fused_computation.4 | custom fusion | flops 256 | bytes 4096 | tf_op jit(solution)/shard_map/scatter-add | solution.py:51
  103.0 2.8 %fusion.473 = f32[131072]{0:T(1024)} fusion(f32[131072]{0:T(1024)} %bitcast.433, s32[]{:T(128)} %bitcast.19, f32[1,1]{1,0:T(1,128)} %get-tuple-element.106, s32[1]{0:T(128)S(6)} %copy.23, s32[1]{0:T(128)} %bitcast.18), kind=kLoop, calls=%fused_computation.781 | loop fusion | flops 14 | bytes 2564 | tf_op jit(solution)/shard_map/scatter-add | solution.py:51
  108.9 2.9 %collective-permute-start.11 = (f32[2,4,64,128]{3,2,1,0:T(8,128)S(1)}, f32[2,4,64,128]{3,2,1,0:T(8,128)S(1)}, u32[]{:S(2)}, u32[]{:S(2)}) collective-permute-start(f32[2,4,64,128]{3,2,1,0:T(8,128)S(1)} %get-tuple-element.75), channel_id=1, source_target_pairs={{0,2},{2,4},{4,6},{6,8},{8,10},{10,12},{12,14},{14,16},{16,18},{18... | collective-permute-start | bytes 786440 | tf_op jit(solution)/shard_map/ppermute | solution.py:19
  112.7 4.8 %collective-permute-done.11 = f32[2,4,64,128]{3,2,1,0:T(8,128)S(1)} collective-permute-done((f32[2,4,64,128]{3,2,1,0:T(8,128)S(1)}, f32[2,4,64,128]{3,2,1,0:T(8,128)S(1)}, u32[]{:S(2)}, u32[]{:S(2)}) %collective-permute-start.11) | collective-permute-done | bytes 262176 | tf_op jit(solution)/shard_map/ppermute | solution.py:19
  119.4 2.1 %fusion.181 = f32[16,64,128]{2,1,0:T(8,128)} fusion(f32[16,64,128]{2,1,0:T(8,128)S(1)} %bitcast.412, f32[16,64,128]{2,1,0:T(8,128)S(1)} %bitcast.436, f32[2,20,64,128]{3,2,1,0:T(8,128)S(1)} %get-tuple-element.73, f32[2,20,64,128]{3,2,1,0:T(8,128)S(1)} %get-tuple-element.72, f32[16,64,128]{2,1,0:T(8,128)S(1)} %bitcast.395, f32[16,64,128]{2,1,0:T(8,128)S(1)} %copy-done.19, ...), kind=kLoop, calls=%fused_computation.417 | loop fusion | flops 6291456 | bytes 11010048 | tf_op jit(solution)/shard_map/add | solution.py:79
  121.5 3.6 %fusion.199 = f32[16,64,128]{2,1,0:T(8,128)S(1)} fusion(f32[16,64,128]{2,1,0:T(8,128)S(1)} %bitcast.413, f32[2,20,64,128]{3,2,1,0:T(8,128)} %copy-done.2, f32[2,20,64,128]{3,2,1,0:T(8,128)} %copy-done.1, f32[16,64,128]{2,1,0:T(8,128)S(1)} %bitcast.396, f32[16,64,128]{2,1,0:T(8,128)S(1)} %copy-done), kind=kLoop, calls=%fused_computation.435 | loop fusion | flops 5505024 | bytes 6291456 | tf_op jit(solution)/shard_map/add | solution.py:81
  125.1 2.5 %scatter_fusion.5 = f32[131072]{0:T(1024)S(1)} fusion(f32[131072]{0:T(1024)S(1)} %bitcast.439, s32[256]{0:T(256)S(1)} %bitcast.446, f32[256]{0:T(256)S(1)} %get-tuple-element.100), kind=kCustom, calls=%fused_computation.5 | custom fusion | flops 256 | bytes 4096 | tf_op jit(solution)/shard_map/scatter-add | solution.py:51
  127.6 8.6 %reduce-scatter.2.cloned.1.call-done = f32[16,32,128]{2,1,0:T(8,128)} async-done(((f32[16,64,128]{2,1,0:T(8,128)}), f32[16,32,128]{2,1,0:T(8,128)}) %reduce-scatter.2.cloned.1.call-update) | async-done | bytes 262160 | tf_op jit(solution)/shard_map/reduce_scatter | solution.py:84
  (87 shorter events, 30.9 us)
Async XLA Ops:
  7.2 129.0 %reduce-scatter.2.cloned.1.call-start = ((), (), s32[]{:S(2)}) async-start(), calls=%async_computation.1 | async-start | bytes 786432 | tf_op jit(solution)/shard_map/reduce_scatter | solution.py:84
  8.4 4.6 %copy-start.24 = (s32[1,256]{1,0:T(1,128)S(1)}, s32[1,256]{1,0:T(1,128)}, u32[]{:S(2)}) copy-start(s32[1,256]{1,0:T(1,128)} %param.26) | copy-start | bytes 3076
  8.4 4.7 %copy-start.23 = (f32[1,6,256]{2,0,1:T(1,128)S(1)}, f32[1,6,256]{2,0,1:T(1,128)}, u32[]{:S(2)}) copy-start(f32[1,6,256]{2,0,1:T(1,128)} %param.27) | copy-start | bytes 18436
  8.4 4.7 %copy-start.22 = (f32[1,6]{1,0:T(1,128)S(1)}, f32[1,6]{1,0:T(1,128)}, u32[]{:S(2)}) copy-start(f32[1,6]{1,0:T(1,128)} %param.24) | copy-start | bytes 76
  8.4 11.7 %copy-start = (f32[16,64,128]{2,1,0:T(8,128)S(1)}, f32[16,64,128]{2,1,0:T(8,128)}, u32[]{:S(2)}) copy-start(f32[16,64,128]{2,1,0:T(8,128)} %param.19) | copy-start | bytes 1572868
  8.4 11.7 %copy-start.9 = (f32[1,16,64,128]{3,2,1,0:T(8,128)S(1)}, f32[1,16,64,128]{3,2,1,0:T(8,128)}, u32[]{:S(2)}) copy-start(f32[1,16,64,128]{3,2,1,0:T(8,128)} %param.20) | copy-start | bytes 1572868
  8.5 6.5 %collective-permute-start = (f32[2,4,64,128]{3,2,1,0:T(8,128)S(1)}, f32[2,4,64,128]{3,2,1,0:T(8,128)S(1)}, u32[]{:S(2)}, u32[]{:S(2)}) collective-permute-start(f32[2,4,64,128]{3,2,1,0:T(8,128)S(1)} %get-tuple-element.92), channel_id=1, source_target_pairs={{2,0},{4,2},{6,4},{8,6},{10,8},{12,10},{14,12},{16,14},{18,16},{20... | collective-permute-start | bytes 786440 | tf_op jit(solution)/shard_map/ppermute | solution.py:20
  10.6 9.5 %collective-permute-start.1 = (f32[2,4,64,128]{3,2,1,0:T(8,128)S(1)}, f32[2,4,64,128]{3,2,1,0:T(8,128)S(1)}, u32[]{:S(2)}, u32[]{:S(2)}) collective-permute-start(f32[2,4,64,128]{3,2,1,0:T(8,128)S(1)} %get-tuple-element.93), channel_id=1, source_target_pairs={{0,2},{2,4},{4,6},{6,8},{8,10},{10,12},{12,14},{14,16},{16,18},{18... | collective-permute-start | bytes 786440 | tf_op jit(solution)/shard_map/ppermute | solution.py:19
  20.1 3.7 %copy-start.20 = (f32[2,4,64,128]{3,2,1,0:T(8,128)}, f32[2,4,64,128]{3,2,1,0:T(8,128)S(1)}, u32[]{:S(2)}) copy-start(f32[2,4,64,128]{3,2,1,0:T(8,128)S(1)} %collective-permute-done.1) | copy-start | bytes 786436
  20.1 5.3 %copy-start.11 = (f32[1,16,64,128]{3,2,1,0:T(8,128)S(1)}, f32[1,16,64,128]{3,2,1,0:T(8,128)}, u32[]{:S(2)}) copy-start(f32[1,16,64,128]{3,2,1,0:T(8,128)} %param.22) | copy-start | bytes 1572868
  20.1 5.3 %copy-start.21 = (f32[1,16,64,128]{3,2,1,0:T(8,128)S(1)}, f32[1,16,64,128]{3,2,1,0:T(8,128)}, u32[]{:S(2)}) copy-start(f32[1,16,64,128]{3,2,1,0:T(8,128)} %param.23) | copy-start | bytes 1572868
  30.2 5.8 %collective-permute-start.2 = (f32[2,4,64,128]{3,2,1,0:T(8,128)S(1)}, f32[2,4,64,128]{3,2,1,0:T(8,128)S(1)}, u32[]{:S(2)}, u32[]{:S(2)}) collective-permute-start(f32[2,4,64,128]{3,2,1,0:T(8,128)S(1)} %get-tuple-element.90), channel_id=1, source_target_pairs={{2,0},{4,2},{6,4},{8,6},{10,8},{12,10},{14,12},{16,14},{18,16},{20... | collective-permute-start | bytes 786440 | tf_op jit(solution)/shard_map/ppermute | solution.py:20
  32.2 8.9 %copy-start.12 = (f32[1,16,64,128]{3,2,1,0:T(8,128)S(1)}, f32[1,16,64,128]{3,2,1,0:T(8,128)}, u32[]{:S(2)}) copy-start(f32[1,16,64,128]{3,2,1,0:T(8,128)} %param.22) | copy-start | bytes 1572868
  32.2 8.6 %collective-permute-start.3 = (f32[2,4,64,128]{3,2,1,0:T(8,128)S(1)}, f32[2,4,64,128]{3,2,1,0:T(8,128)S(1)}, u32[]{:S(2)}, u32[]{:S(2)}) collective-permute-start(f32[2,4,64,128]{3,2,1,0:T(8,128)S(1)} %get-tuple-element.91), channel_id=1, source_target_pairs={{0,2},{2,4},{4,6},{6,8},{8,10},{10,12},{12,14},{14,16},{16,18},{18... | collective-permute-start | bytes 786440 | tf_op jit(solution)/shard_map/ppermute | solution.py:19
  45.6 13.2 %copy-start.3 = (f32[131072]{0:T(1024)}, f32[131072]{0:T(1024)S(1)}, u32[]{:S(2)}) copy-start(f32[131072]{0:T(1024)S(1)} %fusion.470) | copy-start | bytes 1572868
  48.2 5.8 %collective-permute-start.4 = (f32[2,4,64,128]{3,2,1,0:T(8,128)S(1)}, f32[2,4,64,128]{3,2,1,0:T(8,128)S(1)}, u32[]{:S(2)}, u32[]{:S(2)}) collective-permute-start(f32[2,4,64,128]{3,2,1,0:T(8,128)S(1)} %get-tuple-element.86), channel_id=1, source_target_pairs={{2,0},{4,2},{6,4},{8,6},{10,8},{12,10},{14,12},{16,14},{18,16},{20... | collective-permute-start | bytes 786440 | tf_op jit(solution)/shard_map/ppermute | solution.py:20
  50.1 8.7 %collective-permute-start.5 = (f32[2,4,64,128]{3,2,1,0:T(8,128)S(1)}, f32[2,4,64,128]{3,2,1,0:T(8,128)S(1)}, u32[]{:S(2)}, u32[]{:S(2)}) collective-permute-start(f32[2,4,64,128]{3,2,1,0:T(8,128)S(1)} %get-tuple-element.87), channel_id=1, source_target_pairs={{0,2},{2,4},{4,6},{6,8},{8,10},{10,12},{12,14},{14,16},{16,18},{18... | collective-permute-start | bytes 786440 | tf_op jit(solution)/shard_map/ppermute | solution.py:19
  66.5 5.8 %collective-permute-start.6 = (f32[2,4,64,128]{3,2,1,0:T(8,128)S(1)}, f32[2,4,64,128]{3,2,1,0:T(8,128)S(1)}, u32[]{:S(2)}, u32[]{:S(2)}) collective-permute-start(f32[2,4,64,128]{3,2,1,0:T(8,128)S(1)} %get-tuple-element.82), channel_id=1, source_target_pairs={{2,0},{4,2},{6,4},{8,6},{10,8},{12,10},{14,12},{16,14},{18,16},{20... | collective-permute-start | bytes 786440 | tf_op jit(solution)/shard_map/ppermute | solution.py:20
  68.4 8.6 %collective-permute-start.7 = (f32[2,4,64,128]{3,2,1,0:T(8,128)S(1)}, f32[2,4,64,128]{3,2,1,0:T(8,128)S(1)}, u32[]{:S(2)}, u32[]{:S(2)}) collective-permute-start(f32[2,4,64,128]{3,2,1,0:T(8,128)S(1)} %get-tuple-element.83), channel_id=1, source_target_pairs={{0,2},{2,4},{4,6},{6,8},{8,10},{10,12},{12,14},{14,16},{16,18},{18... | collective-permute-start | bytes 786440 | tf_op jit(solution)/shard_map/ppermute | solution.py:19
  85.2 11.7 %copy-start.7 = (f32[131072]{0:T(1024)S(1)}, f32[131072]{0:T(1024)}, u32[]{:S(2)}) copy-start(f32[131072]{0:T(1024)} %copy-done.6) | copy-start | bytes 1572868
  86.3 5.8 %collective-permute-start.8 = (f32[2,4,64,128]{3,2,1,0:T(8,128)S(1)}, f32[2,4,64,128]{3,2,1,0:T(8,128)S(1)}, u32[]{:S(2)}, u32[]{:S(2)}) collective-permute-start(f32[2,4,64,128]{3,2,1,0:T(8,128)S(1)} %get-tuple-element.78), channel_id=1, source_target_pairs={{2,0},{4,2},{6,4},{8,6},{10,8},{12,10},{14,12},{16,14},{18,16},{20... | collective-permute-start | bytes 786440 | tf_op jit(solution)/shard_map/ppermute | solution.py:20
  88.2 8.7 %collective-permute-start.9 = (f32[2,4,64,128]{3,2,1,0:T(8,128)S(1)}, f32[2,4,64,128]{3,2,1,0:T(8,128)S(1)}, u32[]{:S(2)}, u32[]{:S(2)}) collective-permute-start(f32[2,4,64,128]{3,2,1,0:T(8,128)S(1)} %get-tuple-element.79), channel_id=1, source_target_pairs={{0,2},{2,4},{4,6},{6,8},{8,10},{10,12},{12,14},{14,16},{16,18},{18... | collective-permute-start | bytes 786440 | tf_op jit(solution)/shard_map/ppermute | solution.py:19
  105.8 11.7 %copy-start.8 = (f32[131072]{0:T(1024)S(1)}, f32[131072]{0:T(1024)}, u32[]{:S(2)}) copy-start(f32[131072]{0:T(1024)} %fusion.473) | copy-start | bytes 1572868
  106.9 5.8 %collective-permute-start.10 = (f32[2,4,64,128]{3,2,1,0:T(8,128)S(1)}, f32[2,4,64,128]{3,2,1,0:T(8,128)S(1)}, u32[]{:S(2)}, u32[]{:S(2)}) collective-permute-start(f32[2,4,64,128]{3,2,1,0:T(8,128)S(1)} %get-tuple-element.74), channel_id=1, source_target_pairs={{2,0},{4,2},{6,4},{8,6},{10,8},{12,10},{14,12},{16,14},{18,16},{20... | collective-permute-start | bytes 786440 | tf_op jit(solution)/shard_map/ppermute | solution.py:20
  108.8 10.5 %copy-start.13 = (f32[1,16,64,128]{3,2,1,0:T(8,128)S(1)}, f32[1,16,64,128]{3,2,1,0:T(8,128)}, u32[]{:S(2)}) copy-start(f32[1,16,64,128]{3,2,1,0:T(8,128)} %param.22) | copy-start | bytes 1572868
  108.8 10.5 %copy-start.15 = (f32[16,64,128]{2,1,0:T(8,128)S(1)}, f32[16,64,128]{2,1,0:T(8,128)}, u32[]{:S(2)}) copy-start(f32[16,64,128]{2,1,0:T(8,128)} %get-tuple-element.71) | copy-start | bytes 1572868
  108.9 10.5 %copy-start.16 = (f32[16,64,128]{2,1,0:T(8,128)S(1)}, f32[16,64,128]{2,1,0:T(8,128)}, u32[]{:S(2)}) copy-start(f32[16,64,128]{2,1,0:T(8,128)} %get-tuple-element.69) | copy-start | bytes 1572868
  108.9 10.5 %copy-start.17 = (f32[16,64,128]{2,1,0:T(8,128)S(1)}, f32[16,64,128]{2,1,0:T(8,128)}, u32[]{:S(2)}) copy-start(f32[16,64,128]{2,1,0:T(8,128)} %get-tuple-element.67) | copy-start | bytes 1572868
  108.9 10.5 %copy-start.18 = (f32[16,64,128]{2,1,0:T(8,128)S(1)}, f32[16,64,128]{2,1,0:T(8,128)}, u32[]{:S(2)}) copy-start(f32[16,64,128]{2,1,0:T(8,128)} %get-tuple-element.65) | copy-start | bytes 1572868
  108.9 10.5 %copy-start.19 = (f32[16,64,128]{2,1,0:T(8,128)S(1)}, f32[16,64,128]{2,1,0:T(8,128)}, u32[]{:S(2)}) copy-start(f32[16,64,128]{2,1,0:T(8,128)} %get-tuple-element.63) | copy-start | bytes 1572868
  108.9 8.6 %collective-permute-start.11 = (f32[2,4,64,128]{3,2,1,0:T(8,128)S(1)}, f32[2,4,64,128]{3,2,1,0:T(8,128)S(1)}, u32[]{:S(2)}, u32[]{:S(2)}) collective-permute-start(f32[2,4,64,128]{3,2,1,0:T(8,128)S(1)} %get-tuple-element.75), channel_id=1, source_target_pairs={{0,2},{2,4},{4,6},{6,8},{8,10},{10,12},{12,14},{14,16},{16,18},{18... | collective-permute-start | bytes 786440 | tf_op jit(solution)/shard_map/ppermute | solution.py:19
  127.6 10.3 %copy-start.14 = (f32[131072]{0:T(1024)}, f32[131072]{0:T(1024)S(1)}, u32[]{:S(2)}) copy-start(f32[131072]{0:T(1024)S(1)} %scatter_fusion.5) | copy-start | bytes 1572868
  (6 other events, 6.9 us)
Sparse Core Ops, SparseCore 0:
  121.6 14.5 reduce-scatter.1
where the time goes:
time: 147 us; the launch traced here: 145 us
  other arithmetic  53.8 us (37%)
  waiting for transfers between devices  44.1 us (30%)
  starting transfers between devices  26.7 us (18%)
  between operations  15.8 us (11%)
  local copies, waits for them, and re-layouts  4.25 us (3%)
    ppermute x6, waiting for transfers between devices, extended(): before = lax.ppermute(last, axis, up)  29 us
    scatter-add x11, other arithmetic, inject_local(): flat.at[jnp.where(inside, local, 0)].add(jnp.where(inside, values, 0.0))  23.8 us
    ppermute x6, starting transfers between devices, extended(): before = lax.ppermute(last, axis, up)  15.1 us
    add x5, other arithmetic, body(): 2.0 * pc - pn + speed2 * lp  11.7 us
    ppermute x6, starting transfers between devices, extended(): after = lax.ppermute(leading, axis, down)  11.7 us
    add x6, other arithmetic, body(): 2.0 * qc - qn + speed2 * lq  10.7 us
    reduce_scatter x1, waiting for transfers between devices, body(): summed = lax.psum_scatter(grad, 'shot', scatter_dimension=1, tiled=True)  8.59 us
    ppermute x6, waiting for transfers between devices, extended(): after = lax.ppermute(leading, axis, down)  6.58 us
  transfers between devices with their start and end apart: 13, of which 12 were waited for; matrix products, arithmetic and copies ran while one was open for 5% of the time, Pallas kernels for 0%

commit v1 on v0

v1 whole, which is shorter than its diff:
```python
import functools

import jax
import jax.numpy as jnp
import ml_dtypes
import numpy as np
from jax import lax
from jax.experimental import pallas as pl
from jax.experimental.pallas import tpu as pltpu
from jax.sharding import PartitionSpec as P

STEPS = 6
WIDTH = 4
PAD = 8

coefs = (-205.0 / 72.0, 8.0 / 5.0, -1.0 / 5.0, 8.0 / 315.0, -1.0 / 560.0)


def band(depth):
    whole = np.zeros((depth, depth), np.float32)
    for j in range(1, WIDTH + 1):
        whole += np.float32(coefs[j]) * (np.eye(depth, k=j, dtype=np.float32) + np.eye(depth, k=-j, dtype=np.float32))
    high = whole.astype(ml_dtypes.bfloat16)
    low = (whole - high.astype(np.float32)).astype(ml_dtypes.bfloat16)
    return np.block([[high, low], [high, np.zeros_like(high)]])


def split(value, terms):
    parts = []
    for _ in range(terms):
        part = value.astype(jnp.bfloat16)
        parts.append(part)
        value = value - part.astype(jnp.float32)
    return parts


def kernel(
    count, shots,
    courant, p_current, p_later, q_current, q_later, wavelet, source, receivers, residual, matrix,
    gradient, q_final,
    p_ext, q_ext, speed2, grad, spot, inject, others,
    load_sem, send_sem, recv_sem, share_send, share_recv,
):
    rows, ny, nz = speed2.shape
    me = lax.axis_index("space")
    shot = lax.axis_index("shot")
    odd = lax.rem(me, 2)
    exts = (p_ext, q_ext)
    currents = (p_current, q_current)
    ys = pl.ds(PAD, ny)

    def neighbour(side):
        return me - 1 + 2 * side

    def exists(side):
        return jnp.logical_and(neighbour(side) >= 0, neighbour(side) < count)

    def halo_copy(f, k, side):
        dst = exts[f].at[k + 1, pl.ds((1 - side) * (rows + WIDTH), WIDTH), ys]
        if isinstance(k, int) and k == 0:
            src = currents[f].at[0, pl.ds(side * (rows - WIDTH), WIDTH)]
        else:
            src = exts[f].at[k + 1, pl.ds(WIDTH + side * (rows - WIDTH), WIDTH), ys]
        return pltpu.make_async_remote_copy(
            src_ref=src, dst_ref=dst,
            send_sem=send_sem.at[f, k, side], recv_sem=recv_sem.at[f, k, side],
            device_id={"space": neighbour(side)}, device_id_type=pl.DeviceIdType.MESH,
        )

    def halo_wait(f, k, side):
        @pl.when(exists(side))
        def _():
            here = exts[f].at[k + 1, pl.ds(side * (rows + WIDTH), WIDTH), ys]
            pltpu.make_async_remote_copy(
                src_ref=here, dst_ref=here,
                send_sem=send_sem.at[f, k, 1 - side], recv_sem=recv_sem.at[f, k, 1 - side],
                device_id={"space": neighbour(side)}, device_id_type=pl.DeviceIdType.MESH,
            ).wait_recv()

    def halo_send(f, k, side):
        @pl.when(exists(side))
        def _():
            halo_copy(f, k, side).start()

    slow, fast = odd, 1 - odd

    loads = [
        pltpu.make_async_copy(courant, speed2, load_sem.at[0]),
        pltpu.make_async_copy(p_current.at[0], p_ext.at[1, pl.ds(WIDTH, rows), ys], load_sem.at[1]),
        pltpu.make_async_copy(q_current.at[0], q_ext.at[1, pl.ds(WIDTH, rows), ys], load_sem.at[2]),
        pltpu.make_async_copy(p_later.at[0], p_ext.at[0, pl.ds(WIDTH, rows), ys], load_sem.at[3]),
        pltpu.make_async_copy(q_later.at[0], q_ext.at[0, pl.ds(WIDTH, rows), ys], load_sem.at[4]),
    ]
    for load in loads:
        load.start()

    barrier = pltpu.get_barrier_semaphore()
    for side in (0, 1):
        @pl.when(exists(side))
        def _():
            pl.semaphore_signal(
                barrier, inc=1, device_id={"space": neighbour(side)}, device_id_type=pl.DeviceIdType.MESH
            )
    for d in range(1, shots):
        pl.semaphore_signal(
            barrier, inc=1, device_id={"shot": lax.rem(shot + d, shots)}, device_id_type=pl.DeviceIdType.MESH
        )
    pl.semaphore_wait(
        barrier, exists(0).astype(jnp.int32) + exists(1).astype(jnp.int32) + (shots - 1)
    )
    for f in (0, 1):
        for side in (slow, fast):
            halo_send(f, 0, side)

    for ext in exts:
        edge = jnp.zeros((ext.shape[0] - 1, rows, PAD, nz), jnp.float32)
        ext[1:, WIDTH:WIDTH + rows, 0:PAD, :] = edge
        ext[1:, WIDTH:WIDTH + rows, PAD + ny:PAD + ny + PAD, :] = edge
        outside = jnp.zeros((ext.shape[0] - 1, WIDTH, ny, nz), jnp.float32)
        for side in (0, 1):
            @pl.when(jnp.logical_not(exists(side)))
            def _():
                ext[1:, side * (rows + WIDTH):side * (rows + WIDTH) + WIDTH, PAD:PAD + ny, :] = outside

    shift = nz.bit_length() - 1
    cells = receivers[...]
    cell_row = lax.shift_right_logical(cells, shift) - me * (rows * ny)
    cell_column = jnp.bitwise_and(cells, nz - 1)
    column_hit = lax.broadcasted_iota(jnp.int32, (nz, cells.shape[1]), 0) == cell_column
    values = jnp.concatenate(
        [jnp.where(column_hit, residual[0, k:k + 1, :], 0.0) for k in range(STEPS)], axis=0
    )
    value_parts = split(values, 3)
    block = WIDTH * ny
    for c in range(rows // WIDTH):
        ids = lax.broadcasted_iota(jnp.int32, (block, cells.shape[1]), 0) + c * block
        row_hit = jnp.where(ids == cell_row, 1.0, 0.0).astype(jnp.bfloat16)
        total = None
        for part in value_parts:
            term = lax.dot_general(
                row_hit, part, (((1,), (1,)), ((), ())), preferred_element_type=jnp.float32
            )
            total = term if total is None else total + term
        for k in range(STEPS):
            inject[k, c * WIDTH:(c + 1) * WIDTH] = total[:, k * nz:(k + 1) * nz].reshape(WIDTH, ny, nz)
        flat = (
            (lax.broadcasted_iota(jnp.int32, (WIDTH, ny, nz), 0) + (me * rows + c * WIDTH)) * (ny * nz)
            + lax.broadcasted_iota(jnp.int32, (WIDTH, ny, nz), 1) * nz
            + lax.broadcasted_iota(jnp.int32, (WIDTH, ny, nz), 2)
        )
        spot[c * WIDTH:(c + 1) * WIDTH] = jnp.where(flat == source[0], 1.0, 0.0)
    grad[...] = jnp.zeros_like(grad)
    for load in loads:
        load.wait()
    speed2[...] = speed2[...] * speed2[...]

    def laplace(ext, t, r0):
        here = pl.ds(r0 + WIDTH, WIDTH)
        core = ext[t, here, ys, :]
        pair = jnp.concatenate(split(core, 2), axis=-1).reshape(WIDTH * ny, 2 * nz)
        along_z = jnp.dot(pair, matrix[...], preferred_element_type=jnp.float32)
        total = (along_z[:, :nz] + along_z[:, nz:]).reshape(WIDTH, ny, nz) + 3.0 * coefs[0] * core
        for j in range(1, WIDTH + 1):
            total = total + coefs[j] * (
                (ext[t, pl.ds(r0 + WIDTH + j, WIDTH), ys, :] + ext[t, pl.ds(r0 + WIDTH - j, WIDTH), ys, :])
                + (ext[t, here, pl.ds(PAD + j, ny), :] + ext[t, here, pl.ds(PAD - j, ny), :])
            )
        return core, total

    def p_chunk(k, r0, last):
        core, lap = laplace(p_ext, k + 1, r0)
        own, here = pl.ds(r0, WIDTH), pl.ds(r0 + WIDTH, WIDTH)
        grad[own] += q_ext[k + 1, here, ys, :] * lap
        if not last:
            p_ext[k + 2, here, ys, :] = (
                2.0 * core - p_ext[k, here, ys, :] + speed2[own] * lap + wavelet[0, k] * spot[own]
            )

    def q_chunk(k, r0, last):
        core, lap = laplace(q_ext, k + 1, r0)
        own, here = pl.ds(r0, WIDTH), pl.ds(r0 + WIDTH, WIDTH)
        new = 2.0 * core - q_ext[k, here, ys, :] + speed2[own] * lap + inject[k, own]
        if last:
            q_final[0, own] = new
        else:
            q_ext[k + 2, here, ys, :] = new

    chunks = (p_chunk, q_chunk)

    def step(k, last=False, after_inner=None, after_side=None):
        for f in (0, 1):
            for c in range(1, rows // WIDTH - 1):
                chunks[f](k, c * WIDTH, last)
            if f == 0 and after_inner is not None:
                after_inner()
            for side in (fast, slow):
                halo_wait(f, k, side)
                chunks[f](k, side * (rows - WIDTH), last)
                if not last:
                    halo_send(f, k + 1, side)
                elif f == 0:
                    after_side(side)

    def loop(k, carry):
        step(k)
        return carry

    lax.fori_loop(0, STEPS - 1, loop, 0)

    share = ny // shots

    def share_copy(d, part, start, length):
        target = lax.rem(shot + d, shots)
        return pltpu.make_async_remote_copy(
            src_ref=grad.at[pl.ds(start, length), pl.ds(pl.multiple_of(target * share, share), share)],
            dst_ref=others.at[d - 1, pl.ds(start, length)],
            send_sem=share_send.at[d - 1, part], recv_sem=share_recv.at[d - 1, part],
            device_id={"shot": target}, device_id_type=pl.DeviceIdType.MESH,
        )

    def inner_parts(d):
        return share_copy(d, 2, WIDTH, rows - 2 * WIDTH)

    def side_part(d, side):
        return share_copy(d, side, side * (rows - WIDTH), WIDTH)

    def send_inner():
        for d in range(1, shots):
            inner_parts(d).start()

    def send_side(side):
        for d in range(1, shots):
            side_part(d, side).start()

    step(STEPS - 1, True, send_inner, send_side)

    for d in range(1, shots):
        inner_parts(d).wait()
        for side in (fast, slow):
            side_part(d, side).wait()
    total = grad[:, pl.ds(pl.multiple_of(shot * share, share), share), :]
    for d in range(1, shots):
        total = total + others[d - 1]
    gradient[...] = total * (1.0 / (STEPS * shots))

    for f in (0, 1):
        for side in (0, 1):
            @pl.when(exists(side))
            def _():
                halo_copy(f, 0, side).wait_send()

                def finish(k, carry):
                    halo_copy(f, k, side).wait_send()
                    return carry

                lax.fori_loop(1, STEPS, finish, 0)


def body(courant, p_current, p_later, q_current, q_later, wavelet, source_cell, receiver_cells, residual_data):
    rows, ny, nz = courant.shape
    count, shots = lax.axis_size("space"), lax.axis_size("shot")
    share = ny // shots
    hbm = pl.BlockSpec(memory_space=pl.ANY)
    vmem = pl.BlockSpec(memory_space=pltpu.VMEM)
    smem = pl.BlockSpec(memory_space=pltpu.SMEM)
    cells = rows * ny * nz
    call = pl.pallas_call(
        functools.partial(kernel, count, shots),
        out_shape=(
            jax.ShapeDtypeStruct((rows, share, nz), jnp.float32),
            jax.ShapeDtypeStruct((1, rows, ny, nz), jnp.float32),
        ),
        in_specs=[hbm] * 5 + [smem, smem, vmem, vmem, vmem],
        out_specs=(vmem, vmem),
        scratch_shapes=[
            pltpu.VMEM((STEPS + 1, rows + 2 * WIDTH, ny + 2 * PAD, nz), jnp.float32),
            pltpu.VMEM((STEPS + 1, rows + 2 * WIDTH, ny + 2 * PAD, nz), jnp.float32),
            pltpu.VMEM((rows, ny, nz), jnp.float32),
            pltpu.VMEM((rows, ny, nz), jnp.float32),
            pltpu.VMEM((rows, ny, nz), jnp.float32),
            pltpu.VMEM((STEPS, rows, ny, nz), jnp.float32),
            pltpu.VMEM((max(shots - 1, 1), rows, share, nz), jnp.float32),
            pltpu.SemaphoreType.DMA((5,)),
            pltpu.SemaphoreType.DMA((2, STEPS, 2)),
            pltpu.SemaphoreType.DMA((2, STEPS, 2)),
            pltpu.SemaphoreType.DMA((max(shots - 1, 1), 3)),
            pltpu.SemaphoreType.DMA((max(shots - 1, 1), 3)),
        ],
        compiler_params=pltpu.CompilerParams(
            collective_id=0, has_side_effects=True, vmem_limit_bytes=44 * 1024 * 1024
        ),
        cost_estimate=pl.CostEstimate(
            flops=2 * STEPS * 40 * cells, bytes_accessed=7 * 4 * cells, transcendentals=0
        ),
    )
    return call(
        courant, p_current, p_later, q_current, q_later, wavelet, source_cell, receiver_cells, residual_data,
        jnp.asarray(band(nz)),
    )


def solution(mesh):
    in_specs = (
        P("space", None, None),
        P("shot", "space", None, None),
        P("shot", "space", None, None),
        P("shot", "space", None, None),
        P("shot", "space", None, None),
        P("shot", None),
        P("shot"),
        P("shot", None),
        P("shot", None, None),
    )
    out_specs = (P("space", "shot", None), P("shot", "space", None, None))
    return jax.shard_map(body, mesh=mesh, in_specs=in_specs, out_specs=out_specs, check_vma=False)
```

time: 147 us -> 53.5 us (0.36); the launches traced: 145 us -> 53.1 us
  other arithmetic: 53.8 us -> 0 us
  waiting for transfers between devices: 44.1 us -> 0 us
  Pallas kernels: 0 us -> 43.5 us
  starting transfers between devices: 26.7 us -> 0 us
  between operations: 15.8 us -> 1.31 us
  local copies, waits for them, and re-layouts: 4.25 us -> 8.32 us
    pallas_call x0 -> x1, Pallas kernels: none -> 43.5 us  [body(): call(courant, p_current, p_later, q_current, q_later, wavelet, source_cel...]
    ppermute x12 -> x0, waiting for transfers between devices: 35.5 us -> none  [the longest x6 29 us: extended(): before = lax.ppermute(last, axis, up)]
    ppermute x12 -> x0, starting transfers between devices: 26.7 us -> none  [the longest x6 15.1 us: extended(): before = lax.ppermute(last, axis, up)]
    add x12 -> x0, other arithmetic: 24.4 us -> none  [the longest x5 11.7 us: body(): 2.0 * pc - pn + speed2 * lp]
    scatter-add x11 -> x0, other arithmetic: 23.8 us -> none  [inject_local(): flat.at[jnp.where(inside, local, 0)].add(jnp.where(inside, values, 0.0))]
    reduce_scatter x1 -> x0, waiting for transfers between devices: 8.59 us -> none  [body(): summed = lax.psum_scatter(grad, 'shot', scatter_dimension=1, tiled=True)]
    unnamed x51 -> x19, local copies, waits for them, and re-layouts: 3.5 us -> 8.32 us
    slice x5 -> x0, other arithmetic: 2.23 us -> none  [extended(): leading = lax.slice_in_dim(value, 0, width, axis=dim)]
  transfers between devices with their start and end apart: 13 -> 0, of which waited for: 12 -> 0; matrix products, arithmetic and copies ran while one was open for 5% -> 0% of each run, Pallas kernels for 0% -> 0%
where the time goes in v1:
time: 53.5 us; the launch traced here: 53.1 us
  Pallas kernels  43.5 us (81%)
  local copies, waits for them, and re-layouts  8.32 us (16%)
  between operations  1.31 us (2%)
    pallas_call x1, Pallas kernels, body(): call(courant, p_current, p_later, q_current, q_later, wavelet, source_cel...  43.5 us
    unnamed x19, local copies, waits for them, and re-layouts  8.32 us

profile of v1, /device:TPU:10, one launch (start us, length us, event | category | flops | bytes accessed | tf_op | source)
XLA Modules:
  0.0 53.1 jit_solution(11982565951614183209)
XLA Ops:
  1.3 0.0 copy-start.6
  1.3 0.0 copy-start.7
  1.3 0.7 %copy.12.residual = f32[1,6,256]{2,1,0:T(8,128)S(1)} copy(f32[1,6,256]{2,0,1:T(1,128)} %param.18) | data formatting | bytes 12288 | tf_op args[8]
  2.0 0.0 copy-done.6
  2.0 0.0 copy-done.7
  2.0 0.0 copy-start
  2.0 1.0 %copy-done = f32[16,64,128]{2,1,0:T(8,128)S(1)} copy-done((f32[16,64,128]{2,1,0:T(8,128)S(1)}, f32[16,64,128]{2,1,0:T(8,128)}, u32[]{:S(2)}) %copy-start) | copy-done | bytes 524312
  3.1 0.0 copy-start.1
  3.1 1.0 %copy-done.1 = f32[1,16,64,128]{3,2,1,0:T(8,128)S(1)} copy-done((f32[1,16,64,128]{3,2,1,0:T(8,128)S(1)}, f32[1,16,64,128]{3,2,1,0:T(8,128)}, u32[]{:S(2)}) %copy-start.1) | copy-done | bytes 524312
  4.1 0.0 copy-start.2
  4.1 1.0 %copy-done.2 = f32[1,16,64,128]{3,2,1,0:T(8,128)S(1)} copy-done((f32[1,16,64,128]{3,2,1,0:T(8,128)S(1)}, f32[1,16,64,128]{3,2,1,0:T(8,128)}, u32[]{:S(2)}) %copy-start.2) | copy-done | bytes 524312
  5.1 0.0 copy-start.3
  5.1 1.0 %copy-done.3 = f32[1,16,64,128]{3,2,1,0:T(8,128)S(1)} copy-done((f32[1,16,64,128]{3,2,1,0:T(8,128)S(1)}, f32[1,16,64,128]{3,2,1,0:T(8,128)}, u32[]{:S(2)}) %copy-start.3) | copy-done | bytes 524312
  6.2 0.0 copy-start.4
  6.2 1.0 %copy-done.4 = f32[1,16,64,128]{3,2,1,0:T(8,128)S(1)} copy-done((f32[1,16,64,128]{3,2,1,0:T(8,128)S(1)}, f32[1,16,64,128]{3,2,1,0:T(8,128)}, u32[]{:S(2)}) %copy-start.4) | copy-done | bytes 524312
  7.2 0.0 copy-start.5
  7.2 0.9 %copy-done.5 = bf16[256,256]{1,0:T(8,128)(2,1)S(1)} copy-done((bf16[256,256]{1,0:T(8,128)(2,1)S(1)}, bf16[256,256]{1,0:T(8,128)(2,1)}, u32[]{:S(2)}) %copy-start.5) | copy-done | bytes 131096
  8.1 43.5 %shard_map.113 = (f32[16,32,128]{2,1,0:T(8,128)S(1)}, f32[1,16,64,128]{3,2,1,0:T(8,128)S(1)}) custom-call(f32[16,64,128]{2,1,0:T(8,128)S(1)} %copy-done, f32[1,16,64,128]{3,2,1,0:T(8,128)S(1)} %copy-done.1, f32[1,16,64,128]{3,2,1,0:T(8,128)S(1)} %copy-done.2, f32[1,16,64,128]{3,2,1,0:T(8,128)S(1)} %copy-done.3, f32[1,16,64,128]{3,2,1,0:T(8,128)S(1)} %copy-done.4, ...), custom_call_target="tpu_custom_call" | custom-call | flops 62914560 | bytes 3670016 | tf_op jit(solution)/shard_map/pallas_call | solution.py:296
  51.6 0.7 %copy.16 = f32[16,32,128]{2,1,0:T(8,128)} copy(f32[16,32,128]{2,1,0:T(8,128)S(1)} %get-tuple-element.4) | data formatting | bytes 524288
  52.3 0.8 %copy.17 = f32[1,16,64,128]{3,2,1,0:T(8,128)} copy(f32[1,16,64,128]{3,2,1,0:T(8,128)S(1)} %get-tuple-element.5) | data formatting | bytes 1048576
Async XLA Ops:
  1.3 0.7 %copy-start.6 = (s32[1,256]{1,0:T(1,128)S(1)}, s32[1,256]{1,0:T(1,128)}, u32[]{:S(2)}) copy-start(s32[1,256]{1,0:T(1,128)} %receivers.1) | copy-start | bytes 3076
  1.3 0.7 %copy-start.7 = (f32[1,6]{1,0:T(1,128)S(1)}, f32[1,6]{1,0:T(1,128)}, u32[]{:S(2)}) copy-start(f32[1,6]{1,0:T(1,128)} %wavelet.1) | copy-start | bytes 76
  2.0 1.0 %copy-start = (f32[16,64,128]{2,1,0:T(8,128)S(1)}, f32[16,64,128]{2,1,0:T(8,128)}, u32[]{:S(2)}) copy-start(f32[16,64,128]{2,1,0:T(8,128)} %courant.1) | copy-start | bytes 1572868
  3.1 1.0 %copy-start.1 = (f32[1,16,64,128]{3,2,1,0:T(8,128)S(1)}, f32[1,16,64,128]{3,2,1,0:T(8,128)}, u32[]{:S(2)}) copy-start(f32[1,16,64,128]{3,2,1,0:T(8,128)} %p_current.1) | copy-start | bytes 1572868
  4.1 1.0 %copy-start.2 = (f32[1,16,64,128]{3,2,1,0:T(8,128)S(1)}, f32[1,16,64,128]{3,2,1,0:T(8,128)}, u32[]{:S(2)}) copy-start(f32[1,16,64,128]{3,2,1,0:T(8,128)} %p_later.1) | copy-start | bytes 1572868
  5.1 1.0 %copy-start.3 = (f32[1,16,64,128]{3,2,1,0:T(8,128)S(1)}, f32[1,16,64,128]{3,2,1,0:T(8,128)}, u32[]{:S(2)}) copy-start(f32[1,16,64,128]{3,2,1,0:T(8,128)} %q_current.1) | copy-start | bytes 1572868
  6.2 1.0 %copy-start.4 = (f32[1,16,64,128]{3,2,1,0:T(8,128)S(1)}, f32[1,16,64,128]{3,2,1,0:T(8,128)}, u32[]{:S(2)}) copy-start(f32[1,16,64,128]{3,2,1,0:T(8,128)} %q_later.1) | copy-start | bytes 1572868
  7.2 0.9 %copy-start.5 = (bf16[256,256]{1,0:T(8,128)(2,1)S(1)}, bf16[256,256]{1,0:T(8,128)(2,1)}, u32[]{:S(2)}) copy-start(bf16[256,256]{1,0:T(8,128)(2,1)} %constant.2.clone.matrix) | copy-start | bytes 393220

commit v2 on v1

--- a/solution.py
+++ b/solution.py
@@ -2,8 +2,6 @@
 
 import jax
 import jax.numpy as jnp
-import ml_dtypes
-import numpy as np
 from jax import lax
 from jax.experimental import pallas as pl
 from jax.experimental.pallas import tpu as pltpu
@@ -17,12 +15,16 @@
 
 
 def band(depth):
-    whole = np.zeros((depth, depth), np.float32)
+    apart = jnp.abs(
+        lax.broadcasted_iota(jnp.int32, (depth, depth), 0) - lax.broadcasted_iota(jnp.int32, (depth, depth), 1)
+    )
+    whole = jnp.zeros((depth, depth), jnp.float32)
     for j in range(1, WIDTH + 1):
-        whole += np.float32(coefs[j]) * (np.eye(depth, k=j, dtype=np.float32) + np.eye(depth, k=-j, dtype=np.float32))
-    high = whole.astype(ml_dtypes.bfloat16)
-    low = (whole - high.astype(np.float32)).astype(ml_dtypes.bfloat16)
-    return np.block([[high, low], [high, np.zeros_like(high)]])
+        whole = jnp.where(apart == j, coefs[j], whole)
+    high, low = split(whole, 2)
+    return jnp.concatenate(
+        [jnp.concatenate([high, low], axis=1), jnp.concatenate([high, jnp.zeros_like(high)], axis=1)], axis=0
+    )
 
 
 def split(value, terms):
@@ -36,10 +38,10 @@
 
 def kernel(
     count, shots,
-    courant, p_current, p_later, q_current, q_later, wavelet, source, receivers, residual, matrix,
+    courant, p_current, p_later, q_current, q_later, wavelet, source, receivers, residual,
     gradient, q_final,
-    p_ext, q_ext, speed2, grad, spot, inject, others,
-    load_sem, send_sem, recv_sem, share_send, share_recv,
+    p_ext, q_ext, speed2, grad, spot, inject, others, matrix, summed,
+    load_sem, out_sem, send_sem, recv_sem, share_send, share_recv,
 ):
     rows, ny, nz = speed2.shape
     me = lax.axis_index("space")
@@ -112,6 +114,7 @@
         for side in (slow, fast):
             halo_send(f, 0, side)
 
+    matrix[...] = band(nz)
     for ext in exts:
         edge = jnp.zeros((ext.shape[0] - 1, rows, PAD, nz), jnp.float32)
         ext[1:, WIDTH:WIDTH + rows, 0:PAD, :] = edge
@@ -128,7 +131,7 @@
     cell_column = jnp.bitwise_and(cells, nz - 1)
     column_hit = lax.broadcasted_iota(jnp.int32, (nz, cells.shape[1]), 0) == cell_column
     values = jnp.concatenate(
-        [jnp.where(column_hit, residual[0, k:k + 1, :], 0.0) for k in range(STEPS)], axis=0
+        [jnp.where(column_hit, residual[k], 0.0) for k in range(STEPS)], axis=0
     )
     value_parts = split(values, 3)
     block = WIDTH * ny
@@ -176,14 +179,20 @@
                 2.0 * core - p_ext[k, here, ys, :] + speed2[own] * lap + wavelet[0, k] * spot[own]
             )
 
+    def result_copy(r0):
+        return pltpu.make_async_copy(
+            q_ext.at[STEPS + 1, pl.ds(r0 + WIDTH, WIDTH), ys],
+            q_final.at[0, pl.ds(r0, WIDTH)],
+            out_sem.at[r0 // WIDTH],
+        )
+
     def q_chunk(k, r0, last):
         core, lap = laplace(q_ext, k + 1, r0)
         own, here = pl.ds(r0, WIDTH), pl.ds(r0 + WIDTH, WIDTH)
         new = 2.0 * core - q_ext[k, here, ys, :] + speed2[own] * lap + inject[k, own]
+        q_ext[k + 2, here, ys, :] = new
         if last:
-            q_final[0, own] = new
-        else:
-            q_ext[k + 2, here, ys, :] = new
+            result_copy(r0).start()
 
     chunks = (p_chunk, q_chunk)
 
@@ -241,7 +250,9 @@
     total = grad[:, pl.ds(pl.multiple_of(shot * share, share), share), :]
     for d in range(1, shots):
         total = total + others[d - 1]
-    gradient[...] = total * (1.0 / (STEPS * shots))
+    summed[...] = total * (1.0 / (STEPS * shots))
+    gradient_copy = pltpu.make_async_copy(summed, gradient, load_sem.at[0])
+    gradient_copy.start()
 
     for f in (0, 1):
         for side in (0, 1):
@@ -255,12 +266,16 @@
 
                 lax.fori_loop(1, STEPS, finish, 0)
 
+    for c in range(rows // WIDTH):
+        result_copy(c * WIDTH).wait()
+    gradient_copy.wait()
+
 
 def body(courant, p_current, p_later, q_current, q_later, wavelet, source_cell, receiver_cells, residual_data):
     rows, ny, nz = courant.shape
     count, shots = lax.axis_size("space"), lax.axis_size("shot")
     share = ny // shots
-    hbm = pl.BlockSpec(memory_space=pl.ANY)
+    hbm = pl.BlockSpec(memory_space=pltpu.HBM)
     vmem = pl.BlockSpec(memory_space=pltpu.VMEM)
     smem = pl.BlockSpec(memory_space=pltpu.SMEM)
     cells = rows * ny * nz
@@ -270,32 +285,35 @@
             jax.ShapeDtypeStruct((rows, share, nz), jnp.float32),
             jax.ShapeDtypeStruct((1, rows, ny, nz), jnp.float32),
         ),
-        in_specs=[hbm] * 5 + [smem, smem, vmem, vmem, vmem],
-        out_specs=(vmem, vmem),
+        in_specs=[hbm] * 5 + [smem, smem, vmem, vmem],
+        out_specs=(hbm, hbm),
         scratch_shapes=[
             pltpu.VMEM((STEPS + 1, rows + 2 * WIDTH, ny + 2 * PAD, nz), jnp.float32),
-            pltpu.VMEM((STEPS + 1, rows + 2 * WIDTH, ny + 2 * PAD, nz), jnp.float32),
+            pltpu.VMEM((STEPS + 2, rows + 2 * WIDTH, ny + 2 * PAD, nz), jnp.float32),
             pltpu.VMEM((rows, ny, nz), jnp.float32),
             pltpu.VMEM((rows, ny, nz), jnp.float32),
             pltpu.VMEM((rows, ny, nz), jnp.float32),
             pltpu.VMEM((STEPS, rows, ny, nz), jnp.float32),
             pltpu.VMEM((max(shots - 1, 1), rows, share, nz), jnp.float32),
+            pltpu.VMEM((2 * nz, 2 * nz), jnp.bfloat16),
+            pltpu.VMEM((rows, share, nz), jnp.float32),
             pltpu.SemaphoreType.DMA((5,)),
+            pltpu.SemaphoreType.DMA((rows // WIDTH,)),
             pltpu.SemaphoreType.DMA((2, STEPS, 2)),
             pltpu.SemaphoreType.DMA((2, STEPS, 2)),
             pltpu.SemaphoreType.DMA((max(shots - 1, 1), 3)),
             pltpu.SemaphoreType.DMA((max(shots - 1, 1), 3)),
         ],
         compiler_params=pltpu.CompilerParams(
-            collective_id=0, has_side_effects=True, vmem_limit_bytes=44 * 1024 * 1024
+            collective_id=0, has_side_effects=True, vmem_limit_bytes=60 * 1024 * 1024
         ),
         cost_estimate=pl.CostEstimate(
             flops=2 * STEPS * 40 * cells, bytes_accessed=7 * 4 * cells, transcendentals=0
         ),
     )
     return call(
-        courant, p_current, p_later, q_current, q_later, wavelet, source_cell, receiver_cells, residual_data,
-        jnp.asarray(band(nz)),
+        courant, p_current, p_later, q_current, q_later, wavelet, source_cell, receiver_cells,
+        jnp.swapaxes(residual_data, 0, 1),
     )
 
 

time: 53.5 us -> 48.4 us (0.905)
  local copies, waits for them, and re-layouts: 8.32 us -> 2.53 us
  Pallas kernels: 43.5 us -> 44.3 us
    unnamed x19 -> x4, local copies, waits for them, and re-layouts: 8.32 us -> 2.53 us
    pallas_call x1, Pallas kernels: 43.5 us -> 44.3 us  [body(): call(courant, p_current, p_later, q_current, q_later, wavelet, source_cel...]
where the time goes in v2:
time: 48.4 us; the launch traced here: 48.2 us
  Pallas kernels  44.3 us (92%)
  local copies, waits for them, and re-layouts  2.53 us (5%)
  between operations  1.3 us (3%)
    pallas_call x1, Pallas kernels, body(): call(courant, p_current, p_later, q_current, q_later, wavelet, source_cel...  44.3 us
    unnamed x4, local copies, waits for them, and re-layouts  2.53 us

profile of v2, /device:TPU:10, one launch (start us, length us, event | category | flops | bytes accessed | tf_op | source)
XLA Modules:
  0.0 48.2 jit_solution(722267196953164399)
XLA Ops:
  1.3 44.3 %shard_map.104 = (f32[16,32,128]{2,1,0:T(8,128)}, f32[1,16,64,128]{3,2,1,0:T(8,128)}) custom-call(f32[16,64,128]{2,1,0:T(8,128)} %courant.1, f32[1,16,64,128]{3,2,1,0:T(8,128)} %p_current.1, f32[1,16,64,128]{3,2,1,0:T(8,128)} %p_later.1, f32[1,16,64,128]{3,2,1,0:T(8,128)} %q_current.1, f32[1,16,64,128]{3,2,1,0:T(8,128)} %q_later.1, f32[1,6]{1,0:T(1,128)} %wavelet.1, ...), custom_call_target="tpu_custom_call" | custom-call | flops 62914560 | bytes 3670016 | tf_op jit(solution)/shard_map/pallas_call | solution.py:314
  45.6 0.0 copy-start
  45.6 1.7 %copy.14 = f32[16,32,128]{2,1,0:T(8,128)} copy(f32[16,32,128]{2,1,0:T(8,128)} %get-tuple-element.4) | data formatting | bytes 524288
  47.4 0.0 copy-done
  47.4 0.8 %copy.15 = f32[1,16,64,128]{3,2,1,0:T(8,128)} copy(f32[1,16,64,128]{3,2,1,0:T(8,128)S(1)} %copy-done) | data formatting | bytes 1048576
Async XLA Ops:
  45.6 1.7 %copy-start = (f32[1,16,64,128]{3,2,1,0:T(8,128)S(1)}, f32[1,16,64,128]{3,2,1,0:T(8,128)}, u32[]{:S(2)}) copy-start(f32[1,16,64,128]{3,2,1,0:T(8,128)} %get-tuple-element.5) | copy-start | bytes 1572868

commit v3 on v2

--- a/solution.py
+++ b/solution.py
@@ -40,7 +40,7 @@
     count, shots,
     courant, p_current, p_later, q_current, q_later, wavelet, source, receivers, residual,
     gradient, q_final,
-    p_ext, q_ext, speed2, grad, spot, inject, others, matrix, summed,
+    p_ext, q_ext, halos, speed2, grad, spot, inject, others, matrix, summed,
     load_sem, out_sem, send_sem, recv_sem, share_send, share_recv,
 ):
     rows, ny, nz = speed2.shape
@@ -58,31 +58,23 @@
         return jnp.logical_and(neighbour(side) >= 0, neighbour(side) < count)
 
     def halo_copy(f, k, side):
-        dst = exts[f].at[k + 1, pl.ds((1 - side) * (rows + WIDTH), WIDTH), ys]
         if isinstance(k, int) and k == 0:
             src = currents[f].at[0, pl.ds(side * (rows - WIDTH), WIDTH)]
         else:
             src = exts[f].at[k + 1, pl.ds(WIDTH + side * (rows - WIDTH), WIDTH), ys]
         return pltpu.make_async_remote_copy(
-            src_ref=src, dst_ref=dst,
+            src_ref=src, dst_ref=halos.at[f, k, 1 - side],
             send_sem=send_sem.at[f, k, side], recv_sem=recv_sem.at[f, k, side],
             device_id={"space": neighbour(side)}, device_id_type=pl.DeviceIdType.MESH,
         )
 
     def halo_wait(f, k, side):
-        @pl.when(exists(side))
-        def _():
-            here = exts[f].at[k + 1, pl.ds(side * (rows + WIDTH), WIDTH), ys]
-            pltpu.make_async_remote_copy(
-                src_ref=here, dst_ref=here,
-                send_sem=send_sem.at[f, k, 1 - side], recv_sem=recv_sem.at[f, k, 1 - side],
-                device_id={"space": neighbour(side)}, device_id_type=pl.DeviceIdType.MESH,
-            ).wait_recv()
-
-    def halo_send(f, k, side):
-        @pl.when(exists(side))
-        def _():
-            halo_copy(f, k, side).start()
+        here = halos.at[f, k, side]
+        pltpu.make_async_remote_copy(
+            src_ref=here, dst_ref=here,
+            send_sem=send_sem.at[f, k, 1 - side], recv_sem=recv_sem.at[f, k, 1 - side],
+            device_id={"space": neighbour(side)}, device_id_type=pl.DeviceIdType.MESH,
+        ).wait_recv()
 
     slow, fast = odd, 1 - odd
 
@@ -112,7 +104,9 @@
     )
     for f in (0, 1):
         for side in (slow, fast):
-            halo_send(f, 0, side)
+            @pl.when(exists(side))
+            def _():
+                halo_copy(f, 0, side).start()
 
     matrix[...] = band(nz)
     for ext in exts:
@@ -120,10 +114,8 @@
         ext[1:, WIDTH:WIDTH + rows, 0:PAD, :] = edge
         ext[1:, WIDTH:WIDTH + rows, PAD + ny:PAD + ny + PAD, :] = edge
         outside = jnp.zeros((ext.shape[0] - 1, WIDTH, ny, nz), jnp.float32)
-        for side in (0, 1):
-            @pl.when(jnp.logical_not(exists(side)))
-            def _():
-                ext[1:, side * (rows + WIDTH):side * (rows + WIDTH) + WIDTH, PAD:PAD + ny, :] = outside
+        ext[1:, 0:WIDTH, PAD:PAD + ny, :] = outside
+        ext[1:, rows + WIDTH:rows + 2 * WIDTH, PAD:PAD + ny, :] = outside
 
     shift = nz.bit_length() - 1
     cells = receivers[...]
@@ -179,36 +171,54 @@
                 2.0 * core - p_ext[k, here, ys, :] + speed2[own] * lap + wavelet[0, k] * spot[own]
             )
 
-    def result_copy(r0):
-        return pltpu.make_async_copy(
-            q_ext.at[STEPS + 1, pl.ds(r0 + WIDTH, WIDTH), ys],
-            q_final.at[0, pl.ds(r0, WIDTH)],
-            out_sem.at[r0 // WIDTH],
-        )
-
     def q_chunk(k, r0, last):
         core, lap = laplace(q_ext, k + 1, r0)
         own, here = pl.ds(r0, WIDTH), pl.ds(r0 + WIDTH, WIDTH)
-        new = 2.0 * core - q_ext[k, here, ys, :] + speed2[own] * lap + inject[k, own]
-        q_ext[k + 2, here, ys, :] = new
-        if last:
-            result_copy(r0).start()
+        q_ext[k + 2, here, ys, :] = 2.0 * core - q_ext[k, here, ys, :] + speed2[own] * lap + inject[k, own]
+
+    def add_halo(f, k, side, last):
+        for i in range(WIDTH):
+            r = side * (rows - 1) + (1 - 2 * side) * i
+            lap = None
+            for j in range(i + 1, WIDTH + 1):
+                away = j - i
+                term = coefs[j] * halos[f, k, side, (1 - side) * (WIDTH - away) + side * (away - 1)]
+                lap = term if lap is None else lap + term
+            if f == 0:
+                grad[r] += q_ext[k + 1, r + WIDTH, ys, :] * lap
+            if f == 1 or not last:
+                exts[f][k + 2, r + WIDTH, ys, :] += speed2[r] * lap
+
+    def result_copy(part, r0, length):
+        return pltpu.make_async_copy(
+            q_ext.at[STEPS + 1, pl.ds(r0 + WIDTH, length), ys],
+            q_final.at[0, pl.ds(r0, length)],
+            out_sem.at[part],
+        )
+
+    def result_side(side):
+        return result_copy(side, side * (rows - WIDTH), WIDTH)
+
+    def result_inner():
+        return result_copy(2, WIDTH, rows - 2 * WIDTH)
 
     chunks = (p_chunk, q_chunk)
 
     def step(k, last=False, after_inner=None, after_side=None):
         for f in (0, 1):
-            for c in range(1, rows // WIDTH - 1):
+            for c in range(rows // WIDTH):
                 chunks[f](k, c * WIDTH, last)
-            if f == 0 and after_inner is not None:
-                after_inner()
+            if last:
+                after_inner[f]()
             for side in (fast, slow):
-                halo_wait(f, k, side)
-                chunks[f](k, side * (rows - WIDTH), last)
-                if not last:
-                    halo_send(f, k + 1, side)
-                elif f == 0:
-                    after_side(side)
+                @pl.when(exists(side))
+                def _():
+                    halo_wait(f, k, side)
+                    add_halo(f, k, side, last)
+                    if not last:
+                        halo_copy(f, k + 1, side).start()
+                if last:
+                    after_side[f](side)
 
     def loop(k, carry):
         step(k)
@@ -241,7 +251,11 @@
         for d in range(1, shots):
             side_part(d, side).start()
 
-    step(STEPS - 1, True, send_inner, send_side)
+    step(
+        STEPS - 1, True,
+        (send_inner, lambda: result_inner().start()),
+        (send_side, lambda side: result_side(side).start()),
+    )
 
     for d in range(1, shots):
         inner_parts(d).wait()
@@ -266,9 +280,37 @@
 
                 lax.fori_loop(1, STEPS, finish, 0)
 
-    for c in range(rows // WIDTH):
-        result_copy(c * WIDTH).wait()
+    result_inner().wait()
+    for side in (fast, slow):
+        result_side(side).wait()
     gradient_copy.wait()
+
+
+def copy_kernel(gradient, q_final, gradient_out, q_out, sem):
+    half = q_final.shape[1] // 2
+    copies = [pltpu.make_async_copy(gradient, gradient_out, sem.at[0])] + [
+        pltpu.make_async_copy(q_final.at[0, pl.ds(i * half, half)], q_out.at[0, pl.ds(i * half, half)], sem.at[1 + i])
+        for i in (0, 1)
+    ]
+    for copy in copies:
+        copy.start()
+    for copy in copies:
+        copy.wait()
+
+
+def hand_over(gradient, q_final):
+    hbm = pl.BlockSpec(memory_space=pltpu.HBM)
+    return pl.pallas_call(
+        copy_kernel,
+        out_shape=(
+            jax.ShapeDtypeStruct(gradient.shape, gradient.dtype),
+            jax.ShapeDtypeStruct(q_final.shape, q_final.dtype),
+        ),
+        in_specs=[hbm, hbm],
+        out_specs=(hbm, hbm),
+        scratch_shapes=[pltpu.SemaphoreType.DMA((3,))],
+        compiler_params=pltpu.CompilerParams(vmem_limit_bytes=60 * 1024 * 1024),
+    )(gradient, q_final)
 
 
 def body(courant, p_current, p_later, q_current, q_later, wavelet, source_cell, receiver_cells, residual_data):
@@ -290,6 +332,7 @@
         scratch_shapes=[
             pltpu.VMEM((STEPS + 1, rows + 2 * WIDTH, ny + 2 * PAD, nz), jnp.float32),
             pltpu.VMEM((STEPS + 2, rows + 2 * WIDTH, ny + 2 * PAD, nz), jnp.float32),
+            pltpu.VMEM((2, STEPS, 2, WIDTH, ny, nz), jnp.float32),
             pltpu.VMEM((rows, ny, nz), jnp.float32),
             pltpu.VMEM((rows, ny, nz), jnp.float32),
             pltpu.VMEM((rows, ny, nz), jnp.float32),
@@ -298,7 +341,7 @@
             pltpu.VMEM((2 * nz, 2 * nz), jnp.bfloat16),
             pltpu.VMEM((rows, share, nz), jnp.float32),
             pltpu.SemaphoreType.DMA((5,)),
-            pltpu.SemaphoreType.DMA((rows // WIDTH,)),
+            pltpu.SemaphoreType.DMA((3,)),
             pltpu.SemaphoreType.DMA((2, STEPS, 2)),
             pltpu.SemaphoreType.DMA((2, STEPS, 2)),
             pltpu.SemaphoreType.DMA((max(shots - 1, 1), 3)),
@@ -311,10 +354,11 @@
             flops=2 * STEPS * 40 * cells, bytes_accessed=7 * 4 * cells, transcendentals=0
         ),
     )
-    return call(
+    gradient, q_final = call(
         courant, p_current, p_later, q_current, q_later, wavelet, source_cell, receiver_cells,
         jnp.swapaxes(residual_data, 0, 1),
     )
+    return hand_over(gradient, q_final)
 
 
 def solution(mesh):

time: 48.4 us -> 72 us (1.49)
  Pallas kernels: 44.3 us -> 70 us
  local copies, waits for them, and re-layouts: 2.53 us -> 0 us
    pallas_call x0 -> x1, Pallas kernels: none -> 25 us  [hand_over(): pl.pallas_call(copy_kernel, out_shape=(jax.ShapeDtypeStruct(gradient.shap...]
    unnamed x4 -> x0, local copies, waits for them, and re-layouts: 2.53 us -> none
where the time goes in v3:
time: 72 us; the launch traced here: 71.3 us
  Pallas kernels  70 us (97%)
  between operations  1.29 us (2%)
    pallas_call x1, Pallas kernels, body(): call(courant, p_current, p_later, q_current, q_later, wavelet, source_cel...  45 us
    pallas_call x1, Pallas kernels, hand_over(): pl.pallas_call(copy_kernel, out_shape=(jax.ShapeDtypeStruct(gradient.shap...  25 us

profile of v3, /device:TPU:10, one launch (start us, length us, event | category | flops | bytes accessed | tf_op | source)
XLA Modules:
  0.0 71.3 jit_solution(2168298590548417515)
XLA Ops:
  1.3 45.0 %shard_map.104 = (f32[16,32,128]{2,1,0:T(8,128)}, f32[1,16,64,128]{3,2,1,0:T(8,128)}) custom-call(f32[16,64,128]{2,1,0:T(8,128)} %courant.1, f32[1,16,64,128]{3,2,1,0:T(8,128)} %p_current.1, f32[1,16,64,128]{3,2,1,0:T(8,128)} %p_later.1, f32[1,16,64,128]{3,2,1,0:T(8,128)} %q_current.1, f32[1,16,64,128]{3,2,1,0:T(8,128)} %q_later.1, f32[1,6]{1,0:T(1,128)} %wavelet.1, ...), custom_call_target="tpu_custom_call" | custom-call | flops 62914560 | bytes 3670016 | tf_op jit(solution)/shard_map/pallas_call | solution.py:357
  46.3 25.0 %shard_map.105 = (f32[16,32,128]{2,1,0:T(8,128)}, f32[1,16,64,128]{3,2,1,0:T(8,128)}) custom-call(f32[16,32,128]{2,1,0:T(8,128)} %get-tuple-element.4.gradient, f32[1,16,64,128]{3,2,1,0:T(8,128)} %get-tuple-element.5.q_final), custom_call_target="tpu_custom_call" | custom-call | tf_op jit(solution)/shard_map/pallas_call | solution.py:303

commit v4 on v3

--- a/solution.py
+++ b/solution.py
@@ -117,27 +117,7 @@
         ext[1:, 0:WIDTH, PAD:PAD + ny, :] = outside
         ext[1:, rows + WIDTH:rows + 2 * WIDTH, PAD:PAD + ny, :] = outside
 
-    shift = nz.bit_length() - 1
-    cells = receivers[...]
-    cell_row = lax.shift_right_logical(cells, shift) - me * (rows * ny)
-    cell_column = jnp.bitwise_and(cells, nz - 1)
-    column_hit = lax.broadcasted_iota(jnp.int32, (nz, cells.shape[1]), 0) == cell_column
-    values = jnp.concatenate(
-        [jnp.where(column_hit, residual[k], 0.0) for k in range(STEPS)], axis=0
-    )
-    value_parts = split(values, 3)
-    block = WIDTH * ny
     for c in range(rows // WIDTH):
-        ids = lax.broadcasted_iota(jnp.int32, (block, cells.shape[1]), 0) + c * block
-        row_hit = jnp.where(ids == cell_row, 1.0, 0.0).astype(jnp.bfloat16)
-        total = None
-        for part in value_parts:
-            term = lax.dot_general(
-                row_hit, part, (((1,), (1,)), ((), ())), preferred_element_type=jnp.float32
-            )
-            total = term if total is None else total + term
-        for k in range(STEPS):
-            inject[k, c * WIDTH:(c + 1) * WIDTH] = total[:, k * nz:(k + 1) * nz].reshape(WIDTH, ny, nz)
         flat = (
             (lax.broadcasted_iota(jnp.int32, (WIDTH, ny, nz), 0) + (me * rows + c * WIDTH)) * (ny * nz)
             + lax.broadcasted_iota(jnp.int32, (WIDTH, ny, nz), 1) * nz
@@ -145,9 +125,32 @@
         )
         spot[c * WIDTH:(c + 1) * WIDTH] = jnp.where(flat == source[0], 1.0, 0.0)
     grad[...] = jnp.zeros_like(grad)
-    for load in loads:
+    for load in (loads[0], loads[1], loads[2], loads[3]):
         load.wait()
     speed2[...] = speed2[...] * speed2[...]
+
+    def prepare_injection():
+        shift = nz.bit_length() - 1
+        cells = receivers[...]
+        cell_row = lax.shift_right_logical(cells, shift) - me * (rows * ny)
+        cell_column = jnp.bitwise_and(cells, nz - 1)
+        column_hit = lax.broadcasted_iota(jnp.int32, (nz, cells.shape[1]), 0) == cell_column
+        values = jnp.concatenate(
+            [jnp.where(column_hit, residual[k], 0.0) for k in range(STEPS)], axis=0
+        )
+        value_parts = split(values, 3)
+        block = WIDTH * ny
+        for c in range(rows // WIDTH):
+            ids = lax.broadcasted_iota(jnp.int32, (block, cells.shape[1]), 0) + c * block
+            row_hit = jnp.where(ids == cell_row, 1.0, 0.0).astype(jnp.bfloat16)
+            total = None
+            for part in value_parts:
+                term = lax.dot_general(
+                    row_hit, part, (((1,), (1,)), ((), ())), preferred_element_type=jnp.float32
+                )
+                total = term if total is None else total + term
+            for k in range(STEPS):
+                inject[k, c * WIDTH:(c + 1) * WIDTH] = total[:, k * nz:(k + 1) * nz].reshape(WIDTH, ny, nz)
 
     def laplace(ext, t, r0):
         here = pl.ds(r0 + WIDTH, WIDTH)
@@ -206,6 +209,9 @@
 
     def step(k, last=False, after_inner=None, after_side=None):
         for f in (0, 1):
+            if f == 1 and isinstance(k, int) and k == 0:
+                prepare_injection()
+                loads[4].wait()
             for c in range(rows // WIDTH):
                 chunks[f](k, c * WIDTH, last)
             if last:
@@ -224,7 +230,8 @@
         step(k)
         return carry
 
-    lax.fori_loop(0, STEPS - 1, loop, 0)
+    step(0)
+    lax.fori_loop(1, STEPS - 1, loop, 0)
 
     share = ny // shots
 
@@ -284,33 +291,6 @@
     for side in (fast, slow):
         result_side(side).wait()
     gradient_copy.wait()
-
-
-def copy_kernel(gradient, q_final, gradient_out, q_out, sem):
-    half = q_final.shape[1] // 2
-    copies = [pltpu.make_async_copy(gradient, gradient_out, sem.at[0])] + [
-        pltpu.make_async_copy(q_final.at[0, pl.ds(i * half, half)], q_out.at[0, pl.ds(i * half, half)], sem.at[1 + i])
-        for i in (0, 1)
-    ]
-    for copy in copies:
-        copy.start()
-    for copy in copies:
-        copy.wait()
-
-
-def hand_over(gradient, q_final):
-    hbm = pl.BlockSpec(memory_space=pltpu.HBM)
-    return pl.pallas_call(
-        copy_kernel,
-        out_shape=(
-            jax.ShapeDtypeStruct(gradient.shape, gradient.dtype),
-            jax.ShapeDtypeStruct(q_final.shape, q_final.dtype),
-        ),
-        in_specs=[hbm, hbm],
-        out_specs=(hbm, hbm),
-        scratch_shapes=[pltpu.SemaphoreType.DMA((3,))],
-        compiler_params=pltpu.CompilerParams(vmem_limit_bytes=60 * 1024 * 1024),
-    )(gradient, q_final)
 
 
 def body(courant, p_current, p_later, q_current, q_later, wavelet, source_cell, receiver_cells, residual_data):
@@ -354,11 +334,10 @@
             flops=2 * STEPS * 40 * cells, bytes_accessed=7 * 4 * cells, transcendentals=0
         ),
     )
-    gradient, q_final = call(
+    return call(
         courant, p_current, p_later, q_current, q_later, wavelet, source_cell, receiver_cells,
         jnp.swapaxes(residual_data, 0, 1),
     )
-    return hand_over(gradient, q_final)
 
 
 def solution(mesh):

time: 72 us -> 48.7 us (0.68)
  the two profiles are of different devices: /device:TPU:10 before, /device:TPU:13 now
where the time goes in v4:
time: 48.7 us; the launch traced here: 48.5 us
  Pallas kernels  44.7 us (92%)
  local copies, waits for them, and re-layouts  2.53 us (5%)
  between operations  1.3 us (3%)
    pallas_call x1, Pallas kernels, body(): call(courant, p_current, p_later, q_current, q_later, wavelet, source_cel...  44.7 us
    unnamed x4, local copies, waits for them, and re-layouts  2.53 us

profile of v4, /device:TPU:13, one launch (start us, length us, event | category | flops | bytes accessed | tf_op | source)
XLA Modules:
  0.0 48.5 jit_solution(4356665310335941620)
XLA Ops:
  1.3 44.7 %shard_map.104 = (f32[16,32,128]{2,1,0:T(8,128)}, f32[1,16,64,128]{3,2,1,0:T(8,128)}) custom-call(f32[16,64,128]{2,1,0:T(8,128)} %courant.1, f32[1,16,64,128]{3,2,1,0:T(8,128)} %p_current.1, f32[1,16,64,128]{3,2,1,0:T(8,128)} %p_later.1, f32[1,16,64,128]{3,2,1,0:T(8,128)} %q_current.1, f32[1,16,64,128]{3,2,1,0:T(8,128)} %q_later.1, f32[1,6]{1,0:T(1,128)} %wavelet.1, ...), custom_call_target="tpu_custom_call" | custom-call | flops 62914560 | bytes 3670016 | tf_op jit(solution)/shard_map/pallas_call | solution.py:337
  46.0 0.0 copy-start
  46.0 1.7 %copy.14 = f32[16,32,128]{2,1,0:T(8,128)} copy(f32[16,32,128]{2,1,0:T(8,128)} %get-tuple-element.4) | data formatting | bytes 524288
  47.7 0.0 copy-done
  47.7 0.8 %copy.15 = f32[1,16,64,128]{3,2,1,0:T(8,128)} copy(f32[1,16,64,128]{3,2,1,0:T(8,128)S(1)} %copy-done) | data formatting | bytes 1048576
Async XLA Ops:
  46.0 1.7 %copy-start = (f32[1,16,64,128]{3,2,1,0:T(8,128)S(1)}, f32[1,16,64,128]{3,2,1,0:T(8,128)}, u32[]{:S(2)}) copy-start(f32[1,16,64,128]{3,2,1,0:T(8,128)} %get-tuple-element.5) | copy-start | bytes 1572868

commit v5 on v4

--- a/solution.py
+++ b/solution.py
@@ -40,8 +40,9 @@
     count, shots,
     courant, p_current, p_later, q_current, q_later, wavelet, source, receivers, residual,
     gradient, q_final,
-    p_ext, q_ext, halos, speed2, grad, spot, inject, others, matrix, summed,
+    p_ext, q_ext, halos, passing, speed2, grad, spot, inject, others, matrix, summed,
     load_sem, out_sem, send_sem, recv_sem, share_send, share_recv,
+    row_send, row_recv, pass_send, pass_recv,
 ):
     rows, ny, nz = speed2.shape
     me = lax.axis_index("space")
@@ -77,6 +78,75 @@
         ).wait_recv()
 
     slow, fast = odd, 1 - odd
+
+    level, levels = me // 4, count // 4
+    place = lax.rem(me, 4)
+    apart = jnp.logical_or(place == 0, place == 3)
+    ahead = 2 * odd - 1
+    by_way = odd * ((WIDTH * (level + 1)) // levels) + (1 - odd) * ((WIDTH * (levels - level)) // levels)
+    passed = odd * ((WIDTH * level) // levels) + (1 - odd) * ((WIDTH * (levels - 1 - level)) // levels)
+    behind = me - 4 * ahead
+    passes = jnp.logical_and(apart, jnp.logical_and(behind >= 0, behind < count))
+
+    def row_copy(f, k, i, around):
+        if isinstance(k, int) and k == 0:
+            src = currents[f].at[0, slow * (rows - WIDTH) + i]
+        else:
+            src = exts[f].at[k + 1, WIDTH + slow * (rows - WIDTH) + i, ys]
+        return pltpu.make_async_remote_copy(
+            src_ref=src, dst_ref=passing.at[f, k, i] if around else halos.at[f, k, 1 - slow, i],
+            send_sem=row_send.at[f, k, i], recv_sem=(pass_recv if around else row_recv).at[f, k, i],
+            device_id={"space": me + (4 if around else 1) * ahead}, device_id_type=pl.DeviceIdType.MESH,
+        )
+
+    def pass_copy(f, k, i):
+        return pltpu.make_async_remote_copy(
+            src_ref=passing.at[f, k, i], dst_ref=halos.at[f, k, 1 - slow, i],
+            send_sem=pass_send.at[f, k, i], recv_sem=row_recv.at[f, k, i],
+            device_id={"space": me - 3 * ahead}, device_id_type=pl.DeviceIdType.MESH,
+        )
+
+    def pass_on(f, k):
+        for i in range(WIDTH):
+            @pl.when(jnp.logical_and(passes, i < passed))
+            def _():
+                pltpu.make_async_remote_copy(
+                    src_ref=passing.at[f, k, i], dst_ref=passing.at[f, k, i],
+                    send_sem=row_send.at[f, k, i], recv_sem=pass_recv.at[f, k, i],
+                    device_id={"space": behind}, device_id_type=pl.DeviceIdType.MESH,
+                ).wait_recv()
+                pass_copy(f, k, i).start()
+
+    def send(f, k, by_rows, side):
+        if by_rows:
+            for i in range(WIDTH):
+                @pl.when(i < by_way)
+                def _():
+                    row_copy(f, k, i, True).start()
+
+                @pl.when(i >= by_way)
+                def _():
+                    row_copy(f, k, i, False).start()
+        else:
+            halo_copy(f, k, side).start()
+
+    def arrive(f, k, by_rows, side):
+        if by_rows:
+            for i in range(WIDTH):
+                here = halos.at[f, k, slow, i]
+                pltpu.make_async_remote_copy(
+                    src_ref=here, dst_ref=here, send_sem=row_send.at[f, k, i], recv_sem=row_recv.at[f, k, i],
+                    device_id={"space": me + ahead}, device_id_type=pl.DeviceIdType.MESH,
+                ).wait_recv()
+        else:
+            halo_wait(f, k, side)
+
+    def either(side, work):
+        if side is fast:
+            pl.when(exists(side))(lambda: work(False))
+        else:
+            pl.when(jnp.logical_and(exists(side), apart))(lambda: work(True))
+            pl.when(jnp.logical_and(exists(side), jnp.logical_not(apart)))(lambda: work(False))
 
     loads = [
         pltpu.make_async_copy(courant, speed2, load_sem.at[0]),
@@ -95,18 +165,26 @@
             pl.semaphore_signal(
                 barrier, inc=1, device_id={"space": neighbour(side)}, device_id_type=pl.DeviceIdType.MESH
             )
+    meet = [(apart, me - 3 * ahead)]
+    for way in (-4, 4):
+        meet.append((jnp.logical_and(apart, jnp.logical_and(me + way >= 0, me + way < count)), me + way))
+    for wanted, other in meet:
+        @pl.when(wanted)
+        def _():
+            pl.semaphore_signal(
+                barrier, inc=1, device_id={"space": other}, device_id_type=pl.DeviceIdType.MESH
+            )
     for d in range(1, shots):
         pl.semaphore_signal(
             barrier, inc=1, device_id={"shot": lax.rem(shot + d, shots)}, device_id_type=pl.DeviceIdType.MESH
         )
     pl.semaphore_wait(
         barrier, exists(0).astype(jnp.int32) + exists(1).astype(jnp.int32) + (shots - 1)
+        + sum(wanted.astype(jnp.int32) for wanted, _ in meet)
     )
     for f in (0, 1):
         for side in (slow, fast):
-            @pl.when(exists(side))
-            def _():
-                halo_copy(f, 0, side).start()
+            either(side, lambda by_rows: send(f, 0, by_rows, side))
 
     matrix[...] = band(nz)
     for ext in exts:
@@ -216,13 +294,19 @@
                 chunks[f](k, c * WIDTH, last)
             if last:
                 after_inner[f]()
+            if f == 0:
+                pass_on(1, k)
+            elif not last:
+                pass_on(0, k + 1)
             for side in (fast, slow):
+                either(side, lambda by_rows: arrive(f, k, by_rows, side))
+
                 @pl.when(exists(side))
                 def _():
-                    halo_wait(f, k, side)
                     add_halo(f, k, side, last)
-                    if not last:
-                        halo_copy(f, k + 1, side).start()
+
+                if not last:
+                    either(side, lambda by_rows: send(f, k + 1, by_rows, side))
                 if last:
                     after_side[f](side)
 
@@ -230,6 +314,7 @@
         step(k)
         return carry
 
+    pass_on(0, 0)
     step(0)
     lax.fori_loop(1, STEPS - 1, loop, 0)
 
@@ -275,18 +360,25 @@
     gradient_copy = pltpu.make_async_copy(summed, gradient, load_sem.at[0])
     gradient_copy.start()
 
-    for f in (0, 1):
-        for side in (0, 1):
-            @pl.when(exists(side))
-            def _():
-                halo_copy(f, 0, side).wait_send()
-
-                def finish(k, carry):
-                    halo_copy(f, k, side).wait_send()
-                    return carry
-
-                lax.fori_loop(1, STEPS, finish, 0)
-
+    def sent(f, k, by_rows, side):
+        if by_rows:
+            for i in range(WIDTH):
+                row_copy(f, k, i, False).wait_send()
+        else:
+            halo_copy(f, k, side).wait_send()
+
+    def finish(k, carry=0):
+        for f in (0, 1):
+            for side in (fast, slow):
+                either(side, lambda by_rows: sent(f, k, by_rows, side))
+            for i in range(WIDTH):
+                @pl.when(jnp.logical_and(passes, i < passed))
+                def _():
+                    pass_copy(f, k, i).wait_send()
+        return carry
+
+    finish(0)
+    lax.fori_loop(1, STEPS, finish, 0)
     result_inner().wait()
     for side in (fast, slow):
         result_side(side).wait()
@@ -313,6 +405,7 @@
             pltpu.VMEM((STEPS + 1, rows + 2 * WIDTH, ny + 2 * PAD, nz), jnp.float32),
             pltpu.VMEM((STEPS + 2, rows + 2 * WIDTH, ny + 2 * PAD, nz), jnp.float32),
             pltpu.VMEM((2, STEPS, 2, WIDTH, ny, nz), jnp.float32),
+            pltpu.VMEM((2, STEPS, WIDTH, ny, nz), jnp.float32),
             pltpu.VMEM((rows, ny, nz), jnp.float32),
             pltpu.VMEM((rows, ny, nz), jnp.float32),
             pltpu.VMEM((rows, ny, nz), jnp.float32),
@@ -326,6 +419,10 @@
             pltpu.SemaphoreType.DMA((2, STEPS, 2)),
             pltpu.SemaphoreType.DMA((max(shots - 1, 1), 3)),
             pltpu.SemaphoreType.DMA((max(shots - 1, 1), 3)),
+            pltpu.SemaphoreType.DMA((2, STEPS, WIDTH)),
+            pltpu.SemaphoreType.DMA((2, STEPS, WIDTH)),
+            pltpu.SemaphoreType.DMA((2, STEPS, WIDTH)),
+            pltpu.SemaphoreType.DMA((2, STEPS, WIDTH)),
         ],
         compiler_params=pltpu.CompilerParams(
             collective_id=0, has_side_effects=True, vmem_limit_bytes=60 * 1024 * 1024

time: 48.7 us -> 55.2 us (1.13)
  the two profiles are of different devices: /device:TPU:13 before, /device:TPU:0 now
where the time goes in v5:
time: 55.2 us; the launch traced here: 54.9 us
  Pallas kernels  51.1 us (93%)
  local copies, waits for them, and re-layouts  2.53 us (5%)
  between operations  1.3 us (2%)
    pallas_call x1, Pallas kernels, body(): call(courant, p_current, p_later, q_current, q_later, wavelet, source_cel...  51.1 us
    unnamed x4, local copies, waits for them, and re-layouts  2.53 us

profile of v5, /device:TPU:0, one launch (start us, length us, event | category | flops | bytes accessed | tf_op | source)
XLA Modules:
  0.0 54.9 jit_solution(15032553830373099223)
XLA Ops:
  1.3 51.1 %shard_map.104 = (f32[16,32,128]{2,1,0:T(8,128)}, f32[1,16,64,128]{3,2,1,0:T(8,128)}) custom-call(f32[16,64,128]{2,1,0:T(8,128)} %courant.1, f32[1,16,64,128]{3,2,1,0:T(8,128)} %p_current.1, f32[1,16,64,128]{3,2,1,0:T(8,128)} %p_later.1, f32[1,16,64,128]{3,2,1,0:T(8,128)} %q_current.1, f32[1,16,64,128]{3,2,1,0:T(8,128)} %q_later.1, f32[1,6]{1,0:T(1,128)} %wavelet.1, ...), custom_call_target="tpu_custom_call" | custom-call | flops 62914560 | bytes 3670016 | tf_op jit(solution)/shard_map/pallas_call | solution.py:434
  52.4 0.0 copy-start
  52.4 1.7 %copy.14 = f32[16,32,128]{2,1,0:T(8,128)} copy(f32[16,32,128]{2,1,0:T(8,128)} %get-tuple-element.4) | data formatting | bytes 524288
  54.1 0.0 copy-done
  54.1 0.8 %copy.15 = f32[1,16,64,128]{3,2,1,0:T(8,128)} copy(f32[1,16,64,128]{3,2,1,0:T(8,128)S(1)} %copy-done) | data formatting | bytes 1048576
Async XLA Ops:
  52.4 1.7 %copy-start = (f32[1,16,64,128]{3,2,1,0:T(8,128)S(1)}, f32[1,16,64,128]{3,2,1,0:T(8,128)}, u32[]{:S(2)}) copy-start(f32[1,16,64,128]{3,2,1,0:T(8,128)} %get-tuple-element.5) | copy-start | bytes 1572868

commit v6 on v2

--- a/solution.py
+++ b/solution.py
@@ -202,7 +202,7 @@
                 chunks[f](k, c * WIDTH, last)
             if f == 0 and after_inner is not None:
                 after_inner()
-            for side in (fast, slow):
+            for side in (slow, fast):
                 halo_wait(f, k, side)
                 chunks[f](k, side * (rows - WIDTH), last)
                 if not last:

time: 48.4 us -> 48.7 us (level)
  no operation moved by 1% of the time
where the time goes in v6:
time: 48.7 us; the launch traced here: 48.5 us
  Pallas kernels  44.6 us (92%)
  local copies, waits for them, and re-layouts  2.53 us (5%)
  between operations  1.3 us (3%)
    pallas_call x1, Pallas kernels, body(): call(courant, p_current, p_later, q_current, q_later, wavelet, source_cel...  44.6 us
    unnamed x4, local copies, waits for them, and re-layouts  2.53 us

profile of v6, /device:TPU:10, one launch (start us, length us, event | category | flops | bytes accessed | tf_op | source)
XLA Modules:
  0.0 48.5 jit_solution(6875958002785525252)
XLA Ops:
  1.3 44.6 %shard_map.104 = (f32[16,32,128]{2,1,0:T(8,128)}, f32[1,16,64,128]{3,2,1,0:T(8,128)}) custom-call(f32[16,64,128]{2,1,0:T(8,128)} %courant.1, f32[1,16,64,128]{3,2,1,0:T(8,128)} %p_current.1, f32[1,16,64,128]{3,2,1,0:T(8,128)} %p_later.1, f32[1,16,64,128]{3,2,1,0:T(8,128)} %q_current.1, f32[1,16,64,128]{3,2,1,0:T(8,128)} %q_later.1, f32[1,6]{1,0:T(1,128)} %wavelet.1, ...), custom_call_target="tpu_custom_call" | custom-call | flops 62914560 | bytes 3670016 | tf_op jit(solution)/shard_map/pallas_call | solution.py:314
  45.9 0.0 copy-start
  45.9 1.7 %copy.14 = f32[16,32,128]{2,1,0:T(8,128)} copy(f32[16,32,128]{2,1,0:T(8,128)} %get-tuple-element.4) | data formatting | bytes 524288
  47.7 0.0 copy-done
  47.7 0.8 %copy.15 = f32[1,16,64,128]{3,2,1,0:T(8,128)} copy(f32[1,16,64,128]{3,2,1,0:T(8,128)S(1)} %copy-done) | data formatting | bytes 1048576
Async XLA Ops:
  45.9 1.7 %copy-start = (f32[1,16,64,128]{3,2,1,0:T(8,128)S(1)}, f32[1,16,64,128]{3,2,1,0:T(8,128)}, u32[]{:S(2)}) copy-start(f32[1,16,64,128]{3,2,1,0:T(8,128)} %get-tuple-element.5) | copy-start | bytes 1572868
